TPU v7x, 128 devices: a whole 4x4x4 slice. The times are simulated.
128 devices in a mesh: expert: 4 (over y), dp: 32 (over z, x, core).
Axes of the slice: x: 4, y: 4, z: 4, core: 2. Of those that a mesh axis runs over, the one named last changes fastest.
Arguments:
- tokens: bfloat16 [4096, 2048], P(('expert', 'dp')), may hold values from -6 to 6
- expert_ids: int32 [4096, 6], P(('expert', 'dp')), may hold values from 0 to 63, all different within a row; in each aligned block of 32 rows (0 to 31, 32 to 63, ...) at most 4 rows name the same one
- gate_weights: float32 [4096, 6], P(('expert', 'dp')), may hold values from 0.1 to 1
- cotangent: bfloat16 [4096, 2048], P(('expert', 'dp')), may hold values from -6 to 6
- w_gate: bfloat16 [128, 2048, 704], P(('expert', 'dp')), may hold values from -0.125 to 0.125
- w_up: bfloat16 [128, 2048, 704], P(('expert', 'dp')), may hold values from -0.125 to 0.125
- w_down: bfloat16 [128, 704, 2048], P(('expert', 'dp')), may hold values from -0.15625 to 0.15625
Outputs:
- mixed: bfloat16 [4096, 2048], P(('expert', 'dp'))
- d_tokens: bfloat16 [4096, 2048], P(('expert', 'dp'))
- d_gates: float32 [4096, 6], P(('expert', 'dp'))
- g_gate: bfloat16 [128, 2048, 704], P(('expert', 'dp'))
- g_up: bfloat16 [128, 2048, 704], P(('expert', 'dp'))
- g_down: bfloat16 [128, 704, 2048], P(('expert', 'dp'))
Inputs may be any that keep to these rules, and one draw needn't show every extreme that they name: `expert_ids`: within the 32 tokens of one device, each token names 6 different experts, and no expert is named by more than 4 of these tokens; in every draw some device fills some expert's 4 slots.
All inputs are finite; a program needn't handle non-finite values.
Results may differ from a plain program's by a relative error of at most 0.0064.
Values may be sent and summed in bfloat16 or wider, within the bound.
No kernel may reach another device: no remote copies, remote signals or barrier semaphores. Data moves between devices by JAX's collectives and lax.ppermute only.
A program may use at most 128 MiB of HBM per device.

v0:
```python
import functools

import jax
import jax.numpy as jnp
from jax import lax
from jax.experimental import pallas as pl
from jax.experimental.pallas import tpu as pltpu
from jax.sharding import Mesh, PartitionSpec as P

BF16, F32, I32 = jnp.bfloat16, jnp.float32, jnp.int32
CAP = 4
NT = (((1,), (1,)), ((), ()))
TN = (((0,), (0,)), ((), ()))
VMEM = pl.BlockSpec(memory_space=pltpu.VMEM)


def mm(a, b, dims=(((1,), (0,)), ((), ()))):
    return lax.dot_general(a, b, dims, preferred_element_type=F32)


def resident(*arrays):
    return [pltpu.with_memory_space_constraint(a, pltpu.VMEM) for a in arrays]


def routing(ids, gates, first, rows):
    top, toks = ids.shape
    r = lax.broadcasted_iota(I32, (rows, toks), 0) + first
    expert, slot, is_dy = r // (2 * CAP), r % CAP, (r // CAP) % 2 == 1
    chosen = jnp.zeros((rows, toks), F32)
    gate = jnp.zeros((rows, toks), F32)
    for k in range(top):
        same = ids[k : k + 1, :] == expert
        chosen = jnp.where(same, 1.0, chosen)
        gate = jnp.where(same, gates[k : k + 1, :], gate)
    earlier = lax.broadcasted_iota(I32, (toks, toks), 0) < lax.broadcasted_iota(I32, (toks, toks), 1)
    before = mm(chosen.astype(BF16), jnp.where(earlier, 1.0, 0.0).astype(BF16))
    fills = (chosen > 0.5) & (jnp.abs(before - slot.astype(F32)) < 0.5)
    return expert, is_dy, fills, gate


def pack_kernel(ids_ref, gates_ref, tok_ref, cot_ref, out_ref):
    rows = out_ref.shape[0]
    _, is_dy, fills, gate = routing(ids_ref[...], gates_ref[...], pl.program_id(0) * rows, rows)
    pick_x = jnp.where(fills & ~is_dy, 1.0, 0.0)
    pick_dy = jnp.where(fills & is_dy, 1.0, 0.0)
    scale = jnp.sum(pick_x + pick_dy * gate, axis=1, keepdims=True)
    values = mm(pick_x.astype(BF16), tok_ref[...]) + mm(pick_dy.astype(BF16), cot_ref[...])
    out_ref[...] = (values * scale).astype(BF16)


def pack(ids, gates, tokens, cot, experts):
    rows, steps = experts * 2 * CAP, 4
    width = tokens.shape[1]
    whole = lambda a: pl.BlockSpec(a.shape, lambda i: (0, 0))
    return pl.pallas_call(
        pack_kernel,
        grid=(steps,),
        in_specs=[whole(ids), whole(gates), whole(tokens), whole(cot)],
        out_specs=pl.BlockSpec((rows // steps, width), lambda i: (i, 0)),
        out_shape=jax.ShapeDtypeStruct((rows, width), BF16),
        name="pack",
    )(ids, gates, tokens, cot)


def deal(size):
    i = lax.broadcasted_iota(I32, (size, size), 0)
    q = lax.broadcasted_iota(I32, (size, size), 1)
    half = size // 2
    r = i % half
    source = (r // CAP) * 2 * CAP + r % CAP + jnp.where(i >= half, CAP, 0)
    return jnp.where(source == q, 1.0, 0.0).astype(BF16)


def hidden_kernel(z_ref, wg_ref, wu_ref, wd_ref, x_ref, dy_ref, h_ref, dg_ref, du_ref):
    part, cols = 256, 512
    rows, width = z_ref.shape
    hid = wg_ref.shape[0]
    perm = deal(part)
    for m in range(rows // part):
        for n in range(width // cols):
            c = slice(n * cols, (n + 1) * cols)
            dealt = mm(perm, z_ref[m * part : (m + 1) * part, c]).astype(BF16)
            x_ref[m * part // 2 : (m + 1) * part // 2, c] = dealt[: part // 2]
            dy_ref[m * part // 2 : (m + 1) * part // 2, c] = dealt[part // 2 :]
    for lo in range(0, hid, 256):
        s = slice(lo, min(lo + 256, hid))
        g = mm(x_ref[...], wg_ref[s, :], NT)
        u = mm(x_ref[...], wu_ref[s, :], NT)
        dh = mm(dy_ref[...], wd_ref[s, :], NT)
        sig = jax.nn.sigmoid(g)
        act = g * sig
        h_ref[:, s] = (act * u).astype(BF16)
        dg_ref[:, s] = (dh * u * sig * (1.0 + g * (1.0 - sig))).astype(BF16)
        du_ref[:, s] = (dh * act).astype(BF16)


def hidden(z, wg, wu, wd):
    rows, width = z.shape[0] // 2, z.shape[1]
    hid = wg.shape[0]
    out = lambda n: pltpu.VMEM((rows, n), BF16)
    return pl.pallas_call(
        hidden_kernel,
        in_specs=[VMEM] * 4,
        out_specs=[VMEM] * 5,
        out_shape=[out(width), out(width), out(hid), out(hid), out(hid)],
        cost_estimate=pl.CostEstimate(
            flops=6 * rows * width * hid, bytes_accessed=rows * width * 8, transcendentals=rows * hid
        ),
        compiler_params=pltpu.CompilerParams(vmem_limit_bytes=24 << 20),
        name="hidden",
    )(*resident(z, wg, wu, wd))


def project_kernel(h_ref, dg_ref, du_ref, wg_ref, wu_ref, wd_ref, out_ref):
    part, cols = 256, 512
    rows, width = out_ref.shape
    back = deal(part)
    for n in range(width // cols):
        c = slice(n * cols, (n + 1) * cols)
        p = mm(h_ref[...], wd_ref[:, c]).astype(BF16)
        q = (mm(dg_ref[...], wg_ref[:, c]) + mm(du_ref[...], wu_ref[:, c])).astype(BF16)
        for m in range(rows // part):
            r = slice(m * part // 2, (m + 1) * part // 2)
            both = jnp.concatenate([p[r], q[r]], axis=0)
            out_ref[m * part : (m + 1) * part, c] = mm(back, both, TN).astype(BF16)


def project(h, dg, du, wg, wu, wd):
    rows, width, hid = h.shape[0], wg.shape[1], h.shape[1]
    return pl.pallas_call(
        project_kernel,
        in_specs=[VMEM] * 6,
        out_specs=VMEM,
        out_shape=pltpu.VMEM((2 * rows, width), BF16),
        cost_estimate=pl.CostEstimate(
            flops=6 * rows * width * hid, bytes_accessed=rows * width * 8, transcendentals=0
        ),
        compiler_params=pltpu.CompilerParams(vmem_limit_bytes=24 << 20),
        name="project",
    )(*resident(h, dg, du, wg, wu, wd))


def weight_grads_kernel(*refs):
    own, other, outs, turned = refs[:5], refs[5:10], refs[10:13], refs[13]
    rows = own[0].shape[0]

    @pl.when(pl.program_id(0) == 0)
    def _():
        for j, part in enumerate((own, other)):
            for i in range(3):
                turned[i, :, j * rows : (j + 1) * rows] = part[2 + i][...].T

    for i, out in ((0, outs[2]), (1, outs[0]), (2, outs[1])):
        side = 1 if i == 0 else 0
        total = mm(turned[i, :, :rows], own[side][...]) + mm(turned[i, :, rows:], other[side][...])
        out[...] = total.astype(BF16)


def weight_grads(own, other):
    rows, width = own[0].shape
    hid = own[2].shape[1]
    cols = 256
    tall = pl.BlockSpec((rows, cols), lambda i: (0, i))
    whole = pl.BlockSpec((rows, hid), lambda i: (0, 0))
    out = pl.BlockSpec((hid, cols), lambda i: (0, i))
    return pl.pallas_call(
        weight_grads_kernel,
        grid=(width // cols,),
        in_specs=[tall, tall, whole, whole, whole] * 2,
        out_specs=[out] * 3,
        out_shape=[jax.ShapeDtypeStruct((hid, width), BF16)] * 3,
        scratch_shapes=[pltpu.VMEM((3, hid, 2 * rows), BF16)],
        cost_estimate=pl.CostEstimate(
            flops=12 * rows * width * hid, bytes_accessed=6 * hid * width, transcendentals=0
        ),
        compiler_params=pltpu.CompilerParams(vmem_limit_bytes=24 << 20),
        name="weight_grads",
    )(*own, *other)


def combine_kernel(ids_ref, gates_ref, cot_ref, back_ref, mixed_ref, dtok_ref, dgates_ref):
    ids = ids_ref[...]
    rows = back_ref.shape[0]
    expert, is_dy, fills, gate = routing(ids, gates_ref[...], 0, rows)
    gated = jnp.where(fills & ~is_dy, gate, 0.0)
    high = gated.astype(BF16)
    low = (gated - high.astype(F32)).astype(BF16)
    pick = jnp.where(fills & is_dy, 1.0, 0.0).astype(BF16)
    back = back_ref[...]
    mixed_ref[...] = (mm(high, back, TN) + mm(low, back, TN)).astype(BF16)
    dtok_ref[...] = mm(pick, back, TN).astype(BF16)
    inner = jnp.where(fills & ~is_dy, mm(back, cot_ref[...], NT), 0.0)
    for k in range(ids.shape[0]):
        dgates_ref[k : k + 1, :] = jnp.sum(
            jnp.where(ids[k : k + 1, :] == expert, inner, 0.0), axis=0, keepdims=True
        )


def combine(ids, gates, cot, back):
    return pl.pallas_call(
        combine_kernel,
        in_specs=[VMEM] * 4,
        out_specs=[VMEM] * 3,
        out_shape=[
            jax.ShapeDtypeStruct(cot.shape, BF16),
            jax.ShapeDtypeStruct(cot.shape, BF16),
            jax.ShapeDtypeStruct(ids.shape, F32),
        ],
        compiler_params=pltpu.CompilerParams(vmem_limit_bytes=32 << 20),
        name="combine",
    )(ids, gates, cot, *resident(back))


def route(rows):
    chips = lax.axis_size(("expert", "chip"))
    width = rows.shape[1]
    blocks = rows.reshape(chips, -1, width)
    return lax.all_to_all(blocks, ("expert", "chip"), 0, 0, tiled=True).reshape(-1, width)


def swap(rows):
    return lax.ppermute(rows, "core", [(0, 1), (1, 0)])


def local(tokens, expert_ids, gate_weights, cotangent, w_gate, w_up, w_down):
    ids, gates = expert_ids.T, gate_weights.T
    experts = lax.axis_size(("expert", "chip"))
    wg, wu, wd = w_gate[0].T, w_up[0].T, w_down[0]
    z = route(pack(ids, gates, tokens, cotangent, experts))
    z_other = swap(z)
    own = hidden(z, wg, wu, wd)
    other = hidden(z_other, wg, wu, wd)
    theirs = swap(project(*other[2:], wg, wu, wd))
    mine = project(*own[2:], wg, wu, wd)
    back = route((mine.astype(F32) + theirs.astype(F32)).astype(BF16))
    grad_gate, grad_up, grad_down = weight_grads(own, other)
    mixed, d_tokens, d_gates = combine(ids, gates, cotangent, back)
    return (mixed, d_tokens, d_gates.T, grad_gate.T[None], grad_up.T[None], grad_down[None])


def solution(mesh):
    outer, inner = mesh.devices.shape
    chips = Mesh(mesh.devices.reshape(outer, inner // 2, 2), ("expert", "chip", "core"))
    split = ("expert", "chip", "core")
    flat, tall = P(split, None), P(split, None, None)
    return jax.shard_map(
        local,
        mesh=chips,
        in_specs=(flat, flat, flat, flat, tall, tall, tall),
        out_specs=(flat, flat, flat, tall, tall, tall),
        check_vma=False,
    )
```

profile of v0, /device:TPU:1, one launch (start us, length us, event | category | flops | bytes accessed | tf_op | source)
XLA Modules:
  0.0 111.7 jit_solution(10846654561366382415)
XLA Ops:
  0.6 0.0 copy-start.1
  0.6 4.6 %pack.1 = bf16[512,2048]{1,0:T(8,128)(2,1)} custom-call(s32[6,32]{1,0:T(8,128)} %bitcast.37, f32[6,32]{1,0:T(8,128)} %bitcast.39, bf16[32,2048]{1,0:T(8,128)(2,1)} %tok_ref.1, bf16[32,2048]{1,0:T(8,128)(2,1)} %cot_ref.3), custom_call_target="tpu_custom_call" | custom-call | tf_op jit(solution)/shard_map/pack/pallas_call | solution.py:55
  5.2 0.0 copy-start
  5.2 40.8 %all_to_all.10 = bf16[64,8,2048]{2,1,0:T(8,128)(2,1)S(1)} all-to-all(bf16[64,8,2048]{2,1,0:T(8,128)(2,1)} %bitcast.41), channel_id=1, replica_groups=mesh['expert'=4,'chip'=16,'core'=2] {'expert','chip'}, dimensions={0} | all-to-all | bytes 4194304 | tf_op jit(solution)/shard_map/all_to_all | solution.py:218
  46.0 2.9 %collective-permute-start = (bf16[512,2048]{1,0:T(8,128)(2,1)S(1)}, bf16[512,2048]{1,0:T(8,128)(2,1)S(1)}, u32[]{:S(2)}, u32[]{:S(2)}) collective-permute-start(bf16[512,2048]{1,0:T(8,128)(2,1)S(1)} %bitcast.35), channel_id=1, source_target_pairs={{0,1},{1,0},{2,3},{3,2},{4,5},{5,4},{6,7},{7,6},{8,9},{9,8},{10,11... | collective-permute-start | bytes 6291464 | tf_op jit(solution)/shard_map/ppermute | solution.py:222
  48.9 3.8 %collective-permute-done.z_ref = bf16[512,2048]{1,0:T(8,128)(2,1)S(1)} collective-permute-done((bf16[512,2048]{1,0:T(8,128)(2,1)S(1)}, bf16[512,2048]{1,0:T(8,128)(2,1)S(1)}, u32[]{:S(2)}, u32[]{:S(2)}) %collective-permute-start) | collective-permute-done | bytes 2097184 | tf_op jit(solution)/shard_map/ppermute | solution.py:222
  52.7 0.0 copy-done.1
  52.7 0.0 copy-done
  52.7 0.0 copy-start.2
  52.7 1.8 %copy-done.2 = bf16[1,704,2048]{2,1,0:T(8,128)(2,1)S(1)} copy-done((bf16[1,704,2048]{2,1,0:T(8,128)(2,1)S(1)}, bf16[1,704,2048]{2,1,0:T(8,128)(2,1)}, u32[]{:S(2)}) %copy-start.2) | copy-done | bytes 2883608
  54.5 3.5 %hidden.3 = (bf16[256,2048]{1,0:T(8,128)(2,1)S(1)}, bf16[256,2048]{1,0:T(8,128)(2,1)S(1)}, bf16[256,704]{1,0:T(8,128)(2,1)S(1)}, bf16[256,704]{1,0:T(8,128)(2,1)S(1)}, bf16[256,704]{1,0:T(8,128)(2,1)S(1)}) custom-call(bf16[512,2048]{1,0:T(8,128)(2,1)S(1)} %collective-permute-done.z_ref, bf16[704,2048]{1,0:T(8,128)(2,1)S(1)} %bitcast.22, ...), custom_call_target="tpu_custom_call" | custom-call | flops 2214592512 | bytes 4194304 | tf_op jit(solution)/shard_map/hidden/pallas_call | solution.py:101
  58.0 0.0 copy-start.16
  58.0 1.0 copy-done.16
  59.0 0.0 copy-start.18
  59.0 1.0 copy-done.18
  60.0 0.0 copy-start.4
  60.0 0.0 copy-start.6
  60.0 3.5 %project.3 = bf16[512,2048]{1,0:T(8,128)(2,1)S(1)} custom-call(bf16[256,704]{1,0:T(8,128)(2,1)S(1)} %get-tuple-element.25.h_ref.refs_7_, bf16[256,704]{1,0:T(8,128)(2,1)S(1)} %get-tuple-element.26.dg_ref.refs_8_, bf16[256,704]{1,0:T(8,128)(2,1)S(1)} %get-tuple-element.27.du_ref.refs_9_, bf16[704,2048]{1,0:T(8,128)(2,1)S(1)} %bitcast.23, ...), custom_call_target="tpu_custom_call" | custom-call | flops 2214592512 | bytes 4194304 | tf_op jit(solution)/shard_map/project/pallas_call | solution.py:130
  63.5 0.0 copy-done.4
  63.5 0.0 copy-done.6
  63.5 0.6 collective-permute-start.1
  64.2 3.5 %hidden.2 = (bf16[256,2048]{1,0:T(8,128)(2,1)S(1)}, bf16[256,2048]{1,0:T(8,128)(2,1)S(1)}, bf16[256,704]{1,0:T(8,128)(2,1)S(1)}, bf16[256,704]{1,0:T(8,128)(2,1)S(1)}, bf16[256,704]{1,0:T(8,128)(2,1)S(1)}) custom-call(bf16[512,2048]{1,0:T(8,128)(2,1)S(1)} %bitcast.36, bf16[704,2048]{1,0:T(8,128)(2,1)S(1)} %bitcast.24, bf16[704,2048]{1,0:T(8,128)(2,1)S(1)} %bitcast.28, ...), custom_call_target="tpu_custom_call" | custom-call | flops 2214592512 | bytes 4194304 | tf_op jit(solution)/shard_map/hidden/pallas_call | solution.py:101
  67.7 0.0 copy-start.8
  67.7 0.0 copy-start.10
  67.7 0.0 copy-start.12
  67.7 0.0 copy-start.20
  67.7 0.0 copy-start.22
  67.7 3.5 %project.2 = bf16[512,2048]{1,0:T(8,128)(2,1)S(1)} custom-call(bf16[256,704]{1,0:T(8,128)(2,1)S(1)} %get-tuple-element.22.h_ref.refs_2_, bf16[256,704]{1,0:T(8,128)(2,1)S(1)} %get-tuple-element.23.dg_ref.refs_3_, bf16[256,704]{1,0:T(8,128)(2,1)S(1)} %get-tuple-element.24.du_ref.refs_4_, bf16[704,2048]{1,0:T(8,128)(2,1)S(1)} %bitcast.25, ...), custom_call_target="tpu_custom_call" | custom-call | flops 2214592512 | bytes 4194304 | tf_op jit(solution)/shard_map/project/pallas_call | solution.py:130
  71.3 0.0 copy-done.8
  71.3 0.0 copy-done.10
  71.3 0.0 copy-done.12
  71.3 0.0 copy-done.20
  71.3 0.0 copy-done.22
  71.3 0.0 collective-permute-done.1
  71.4 2.3 %fusion = bf16[64,8,2048]{2,1,0:T(8,128)(2,1)} fusion(bf16[512,2048]{1,0:T(8,128)(2,1)S(1)} %collective-permute-done.1, bf16[512,2048]{1,0:T(8,128)(2,1)S(1)} %project.2), kind=kLoop, calls=%fused_computation.1 | loop fusion | flops 4194304 | bytes 6291456 | tf_op jit(solution)/shard_map/reshape | solution.py:217
  73.6 0.0 copy-start.5
  73.6 4.8 %all-to-all-start.1 = ((bf16[64,8,2048]{2,1,0:T(8,128)(2,1)}), bf16[64,8,2048]{2,1,0:T(8,128)(2,1)S(1)}, u32[]{:S(2)}, u32[]{:S(2)}) async-start(bf16[64,8,2048]{2,1,0:T(8,128)(2,1)} %fusion), calls=%async_computation.1 | async-start | bytes 4194304 | tf_op jit(solution)/shard_map/all_to_all | solution.py:218
  78.5 0.0 copy-done.5
  78.5 0.0 copy-start.7
  78.5 1.0 copy-done.7
  79.5 0.0 copy-start.9
  79.5 1.0 copy-done.9
  80.5 0.0 copy-start.11
  80.5 1.0 copy-done.11
  81.5 0.0 copy-start.13
  81.5 1.0 copy-done.13
  82.5 0.0 copy-start.17
  82.5 1.2 %copy-done.17 = bf16[256,2048]{1,0:T(8,128)(2,1)S(1)} copy-done((bf16[256,2048]{1,0:T(8,128)(2,1)S(1)}, bf16[256,2048]{1,0:T(8,128)(2,1)}, u32[]{:S(2)}) %copy-start.17) | copy-done | bytes 1048600
  83.7 0.0 copy-start.19
  83.7 1.2 %copy-done.19 = bf16[256,2048]{1,0:T(8,128)(2,1)S(1)} copy-done((bf16[256,2048]{1,0:T(8,128)(2,1)S(1)}, bf16[256,2048]{1,0:T(8,128)(2,1)}, u32[]{:S(2)}) %copy-start.19) | copy-done | bytes 1048600
  84.9 0.0 copy-start.21
  84.9 1.2 %copy-done.21 = bf16[256,2048]{1,0:T(8,128)(2,1)S(1)} copy-done((bf16[256,2048]{1,0:T(8,128)(2,1)S(1)}, bf16[256,2048]{1,0:T(8,128)(2,1)}, u32[]{:S(2)}) %copy-start.21) | copy-done | bytes 1048600
  86.1 0.0 copy-start.23
  86.1 1.2 %copy-done.23 = bf16[256,2048]{1,0:T(8,128)(2,1)S(1)} copy-done((bf16[256,2048]{1,0:T(8,128)(2,1)S(1)}, bf16[256,2048]{1,0:T(8,128)(2,1)}, u32[]{:S(2)}) %copy-start.23) | copy-done | bytes 1048600
  87.4 0.0 copy-start.3
  87.4 0.0 copy-start.14
  87.4 0.0 copy-start.15
  87.4 8.6 %weight_grads.1 = (bf16[704,2048]{1,0:T(8,128)(2,1)}, bf16[704,2048]{1,0:T(8,128)(2,1)}, bf16[704,2048]{1,0:T(8,128)(2,1)}) custom-call(bf16[256,2048]{1,0:T(8,128)(2,1)S(1)} %copy-done.21, bf16[256,2048]{1,0:T(8,128)(2,1)S(1)} %copy-done.23, bf16[256,704]{1,0:T(8,128)(2,1)S(1)} %copy-done.9, bf16[256,704]{1,0:T(8,128)(2,1)S(1)} %copy-done.11, ...), custom_call_target="tpu_custom_call" | custom-call | flops 4429185024 | bytes 8650752 | tf_op jit(solution)/shard_map/weight_grads/pallas_call | solution.py:166
  96.0 12.9 %all-to-all-done.1 = bf16[64,8,2048]{2,1,0:T(8,128)(2,1)S(1)} async-done(((bf16[64,8,2048]{2,1,0:T(8,128)(2,1)}), bf16[64,8,2048]{2,1,0:T(8,128)(2,1)S(1)}, u32[]{:S(2)}, u32[]{:S(2)}) %all-to-all-start.1) | async-done | bytes 2097184 | tf_op jit(solution)/shard_map/all_to_all | solution.py:218
  108.9 0.0 copy-done.3
  108.9 0.0 copy-done.14
  108.9 0.0 copy-done.15
  108.9 2.9 %combine.1 = (bf16[32,2048]{1,0:T(8,128)(2,1)}, bf16[32,2048]{1,0:T(8,128)(2,1)}, f32[6,32]{1,0:T(8,128)}) custom-call(s32[6,32]{1,0:T(8,128)S(1)} %bitcast.38, f32[6,32]{1,0:T(8,128)S(1)} %bitcast.40, bf16[32,2048]{1,0:T(8,128)(2,1)S(1)} %copy-done.3, bf16[512,2048]{1,0:T(8,128)(2,1)S(1)} %bitcast.34), custom_call_target="tpu_custom_call" | custom-call | tf_op jit(solution)/shard_map/combine/pallas_call | solution.py:200
Async XLA Ops:
  0.6 52.0 %copy-start.1 = (bf16[1,2048,704]{1,2,0:T(8,128)(2,1)S(1)}, bf16[1,2048,704]{1,2,0:T(8,128)(2,1)}, u32[]{:S(2)}) copy-start(bf16[1,2048,704]{1,2,0:T(8,128)(2,1)} %param.12) | copy-start | bytes 8650756
  5.2 47.5 %copy-start = (bf16[1,2048,704]{1,2,0:T(8,128)(2,1)S(1)}, bf16[1,2048,704]{1,2,0:T(8,128)(2,1)}, u32[]{:S(2)}) copy-start(bf16[1,2048,704]{1,2,0:T(8,128)(2,1)} %param.11) | copy-start | bytes 8650756
  46.0 6.7 %collective-permute-start = (bf16[512,2048]{1,0:T(8,128)(2,1)S(1)}, bf16[512,2048]{1,0:T(8,128)(2,1)S(1)}, u32[]{:S(2)}, u32[]{:S(2)}) collective-permute-start(bf16[512,2048]{1,0:T(8,128)(2,1)S(1)} %bitcast.35), channel_id=1, source_target_pairs={{0,1},{1,0},{2,3},{3,2},{4,5},{5,4},{6,7},{7,6},{8,9},{9,8},{10,11... | collective-permute-start | bytes 6291464 | tf_op jit(solution)/shard_map/ppermute | solution.py:222
  52.7 1.8 %copy-start.2 = (bf16[1,704,2048]{2,1,0:T(8,128)(2,1)S(1)}, bf16[1,704,2048]{2,1,0:T(8,128)(2,1)}, u32[]{:S(2)}) copy-start(bf16[1,704,2048]{2,1,0:T(8,128)(2,1)} %param.13) | copy-start | bytes 8650756
  58.0 1.0 copy-start.16
  59.0 1.0 copy-start.18
  60.0 3.6 %copy-start.4 = (bf16[256,704]{1,0:T(8,128)(2,1)}, bf16[256,704]{1,0:T(8,128)(2,1)S(1)}, u32[]{:S(2)}) copy-start(bf16[256,704]{1,0:T(8,128)(2,1)S(1)} %get-tuple-element.26.dg_ref.refs_8_) | copy-start | bytes 1081348
  60.0 3.6 %copy-start.6 = (bf16[256,704]{1,0:T(8,128)(2,1)}, bf16[256,704]{1,0:T(8,128)(2,1)S(1)}, u32[]{:S(2)}) copy-start(bf16[256,704]{1,0:T(8,128)(2,1)S(1)} %get-tuple-element.27.du_ref.refs_9_) | copy-start | bytes 1081348
  63.5 7.8 %collective-permute-start.1 = (bf16[512,2048]{1,0:T(8,128)(2,1)S(1)}, bf16[512,2048]{1,0:T(8,128)(2,1)S(1)}, u32[]{:S(2)}, u32[]{:S(2)}) collective-permute-start(bf16[512,2048]{1,0:T(8,128)(2,1)S(1)} %project.3), channel_id=1, source_target_pairs={{0,1},{1,0},{2,3},{3,2},{4,5},{5,4},{6,7},{7,6},{8,9},{9,8},{10,11... | collective-permute-start | bytes 6291464 | tf_op jit(solution)/shard_map/ppermute | solution.py:222
  67.7 3.6 %copy-start.8 = (bf16[256,704]{1,0:T(8,128)(2,1)}, bf16[256,704]{1,0:T(8,128)(2,1)S(1)}, u32[]{:S(2)}) copy-start(bf16[256,704]{1,0:T(8,128)(2,1)S(1)} %get-tuple-element.22.h_ref.refs_2_) | copy-start | bytes 1081348
  67.7 3.6 %copy-start.10 = (bf16[256,704]{1,0:T(8,128)(2,1)}, bf16[256,704]{1,0:T(8,128)(2,1)S(1)}, u32[]{:S(2)}) copy-start(bf16[256,704]{1,0:T(8,128)(2,1)S(1)} %get-tuple-element.23.dg_ref.refs_3_) | copy-start | bytes 1081348
  67.7 3.6 %copy-start.12 = (bf16[256,704]{1,0:T(8,128)(2,1)}, bf16[256,704]{1,0:T(8,128)(2,1)S(1)}, u32[]{:S(2)}) copy-start(bf16[256,704]{1,0:T(8,128)(2,1)S(1)} %get-tuple-element.24.du_ref.refs_4_) | copy-start | bytes 1081348
  67.7 3.6 %copy-start.20 = (bf16[256,2048]{1,0:T(8,128)(2,1)}, bf16[256,2048]{1,0:T(8,128)(2,1)S(1)}, u32[]{:S(2)}) copy-start(bf16[256,2048]{1,0:T(8,128)(2,1)S(1)} %get-tuple-element.31.refs_0_) | copy-start | bytes 3145732
  67.7 3.6 %copy-start.22 = (bf16[256,2048]{1,0:T(8,128)(2,1)}, bf16[256,2048]{1,0:T(8,128)(2,1)S(1)}, u32[]{:S(2)}) copy-start(bf16[256,2048]{1,0:T(8,128)(2,1)S(1)} %get-tuple-element.32.refs_1_) | copy-start | bytes 3145732
  73.6 4.8 %copy-start.5 = (bf16[256,704]{1,0:T(8,128)(2,1)S(1)}, bf16[256,704]{1,0:T(8,128)(2,1)}, u32[]{:S(2)}) copy-start(bf16[256,704]{1,0:T(8,128)(2,1)} %copy-done.4) | copy-start | bytes 1081348
  73.6 35.2 %all-to-all-start.1 = ((bf16[64,8,2048]{2,1,0:T(8,128)(2,1)}), bf16[64,8,2048]{2,1,0:T(8,128)(2,1)S(1)}, u32[]{:S(2)}, u32[]{:S(2)}) async-start(bf16[64,8,2048]{2,1,0:T(8,128)(2,1)} %fusion), calls=%async_computation.1 | async-start | bytes 4194304 | tf_op jit(solution)/shard_map/all_to_all | solution.py:218
  78.5 1.0 copy-start.7
  79.5 1.0 copy-start.9
  80.5 1.0 copy-start.11
  81.5 1.0 copy-start.13
  82.5 1.2 %copy-start.17 = (bf16[256,2048]{1,0:T(8,128)(2,1)S(1)}, bf16[256,2048]{1,0:T(8,128)(2,1)}, u32[]{:S(2)}) copy-start(bf16[256,2048]{1,0:T(8,128)(2,1)} %copy-done.16) | copy-start | bytes 3145732
  83.7 1.2 %copy-start.19 = (bf16[256,2048]{1,0:T(8,128)(2,1)S(1)}, bf16[256,2048]{1,0:T(8,128)(2,1)}, u32[]{:S(2)}) copy-start(bf16[256,2048]{1,0:T(8,128)(2,1)} %copy-done.18) | copy-start | bytes 3145732
  84.9 1.2 %copy-start.21 = (bf16[256,2048]{1,0:T(8,128)(2,1)S(1)}, bf16[256,2048]{1,0:T(8,128)(2,1)}, u32[]{:S(2)}) copy-start(bf16[256,2048]{1,0:T(8,128)(2,1)} %copy-done.20) | copy-start | bytes 3145732
  86.1 1.2 %copy-start.23 = (bf16[256,2048]{1,0:T(8,128)(2,1)S(1)}, bf16[256,2048]{1,0:T(8,128)(2,1)}, u32[]{:S(2)}) copy-start(bf16[256,2048]{1,0:T(8,128)(2,1)} %copy-done.22) | copy-start | bytes 3145732
  87.4 21.5 %copy-start.3 = (bf16[32,2048]{1,0:T(8,128)(2,1)S(1)}, bf16[32,2048]{1,0:T(8,128)(2,1)}, u32[]{:S(2)}) copy-start(bf16[32,2048]{1,0:T(8,128)(2,1)} %cot_ref.3) | copy-start | bytes 393220
  87.4 21.5 %copy-start.14 = (s32[32,6]{0,1:T(8,128)S(1)}, s32[32,6]{0,1:T(8,128)}, u32[]{:S(2)}) copy-start(s32[32,6]{0,1:T(8,128)} %param.8) | copy-start | bytes 2308
  87.4 21.5 %copy-start.15 = (f32[32,6]{0,1:T(8,128)S(1)}, f32[32,6]{0,1:T(8,128)}, u32[]{:S(2)}) copy-start(f32[32,6]{0,1:T(8,128)} %param.9) | copy-start | bytes 2308
where the time goes:
time: 112 us
  blocking collectives  40.8 us (36%)
  Pallas kernels  30.2 us (27%)
  waiting for transfers between devices  16.6 us (15%)
  local copies, waits for them, and re-layouts  12.7 us (11%)
  starting transfers between devices  8.35 us (7%)
  other arithmetic  2.27 us (2%)
    all_to_all x1, blocking collectives, route(): lax.all_to_all(blocks, ('expert', 'chip'), 0, 0, tiled=True)  40.8 us
    all_to_all x1, waiting for transfers between devices, route(): lax.all_to_all(blocks, ('expert', 'chip'), 0, 0, tiled=True)  12.9 us
    unnamed x48, local copies, waits for them, and re-layouts  12.7 us
    pallas_call x1, Pallas kernels, weight_grads(): pl.pallas_call(weight_grads_kernel, grid=(width // cols,), in_specs=[tall...  8.65 us
    pallas_call x2, Pallas kernels, project(): pl.pallas_call(project_kernel, in_specs=[VMEM] * 6, out_specs=VMEM, out_s...  7.09 us
    pallas_call x2, Pallas kernels, hidden(): pl.pallas_call(hidden_kernel, in_specs=[VMEM] * 4, out_specs=[VMEM] * 5,...  7 us
    all_to_all x1, starting transfers between devices, route(): lax.all_to_all(blocks, ('expert', 'chip'), 0, 0, tiled=True)  4.82 us
    pallas_call x1, Pallas kernels, pack(): pl.pallas_call(pack_kernel, grid=(steps,), in_specs=[whole(ids), whole(ga...  4.57 us
  transfers between devices with their start and end apart: 3, of which 2 were waited for; matrix products, arithmetic and copies ran while one was open for 0% of the time, Pallas kernels for 14%

commit v1 on v0

v1 whole, which is shorter than its diff:
```python
import functools

import jax
import jax.numpy as jnp
from jax import lax
from jax.experimental import pallas as pl
from jax.experimental.pallas import tpu as pltpu
from jax.sharding import Mesh, PartitionSpec as P

BF16, F32, I32 = jnp.bfloat16, jnp.float32, jnp.int32
CAP = 4
NT = (((1,), (1,)), ((), ()))
TN = (((0,), (0,)), ((), ()))
VMEM = pl.BlockSpec(memory_space=pltpu.VMEM)
HBM = pl.BlockSpec(memory_space=pltpu.HBM)
ANY = pl.BlockSpec(memory_space=pl.ANY)


def mm(a, b, dims=(((1,), (0,)), ((), ()))):
    return lax.dot_general(a, b, dims, preferred_element_type=F32)


def resident(*arrays):
    return [pltpu.with_memory_space_constraint(a, pltpu.VMEM) for a in arrays]


def routing(ids, gates, first, rows):
    top, toks = ids.shape
    r = lax.broadcasted_iota(I32, (rows, toks), 0) + first
    expert, slot, is_dy = r // (2 * CAP), r % CAP, (r // CAP) % 2 == 1
    chosen = jnp.zeros((rows, toks), F32)
    gate = jnp.zeros((rows, toks), F32)
    for k in range(top):
        same = ids[k : k + 1, :] == expert
        chosen = jnp.where(same, 1.0, chosen)
        gate = jnp.where(same, gates[k : k + 1, :], gate)
    earlier = lax.broadcasted_iota(I32, (toks, toks), 0) < lax.broadcasted_iota(I32, (toks, toks), 1)
    before = mm(chosen.astype(BF16), jnp.where(earlier, 1.0, 0.0).astype(BF16))
    fills = (chosen > 0.5) & (jnp.abs(before - slot.astype(F32)) < 0.5)
    return expert, is_dy, fills, gate


def pack_kernel(ids_ref, gates_ref, tok_ref, cot_ref, out_ref):
    rows = out_ref.shape[0]
    _, is_dy, fills, gate = routing(ids_ref[...], gates_ref[...], pl.program_id(0) * rows, rows)
    pick_x = jnp.where(fills & ~is_dy, 1.0, 0.0)
    pick_dy = jnp.where(fills & is_dy, 1.0, 0.0)
    scale = jnp.sum(pick_x + pick_dy * gate, axis=1, keepdims=True)
    pick = jnp.concatenate([pick_x, pick_dy], axis=1).astype(BF16)
    both = jnp.concatenate([tok_ref[...], cot_ref[...]], axis=0)
    out_ref[...] = (mm(pick, both) * scale).astype(BF16)


def pack(ids, gates, tokens, cot, experts):
    rows, steps = experts * 2 * CAP, 4
    width = tokens.shape[1]
    whole = lambda a: pl.BlockSpec(a.shape, lambda i: (0, 0))
    return pl.pallas_call(
        pack_kernel,
        grid=(steps,),
        in_specs=[whole(ids), whole(gates), whole(tokens), whole(cot)],
        out_specs=pl.BlockSpec((rows // steps, width), lambda i: (i, 0)),
        out_shape=jax.ShapeDtypeStruct((rows, width), BF16),
        name="pack",
    )(ids, gates, tokens, cot)


def deal(size):
    i = lax.broadcasted_iota(I32, (size, size), 0)
    q = lax.broadcasted_iota(I32, (size, size), 1)
    half = size // 2
    r = i % half
    source = (r // CAP) * 2 * CAP + r % CAP + jnp.where(i >= half, CAP, 0)
    return jnp.where(source == q, 1.0, 0.0).astype(BF16)


def expert_kernel(z_ref, wg_ref, wu_ref, wd_hbm, wg2_hbm, wu2_hbm, wd2_hbm, *refs):
    rows_hbm, act_hbm, act2_hbm, sent_hbm = refs[:4]
    w, rows_ref, act, sent, w_sem, out_sem = refs[4:]
    part, tile, cols = 256, 352, 1024
    rows, width = z_ref.shape
    hid = wg_ref.shape[0]
    loads = [
        pltpu.make_async_copy(hbm, w.at[i], w_sem.at[i]) for i, hbm in enumerate((wd_hbm, wg2_hbm, wu2_hbm, wd2_hbm))
    ]
    for load in loads:
        load.start()
    perm = deal(part)
    for m in range(rows // part):
        dealt = mm(perm, z_ref[m * part : (m + 1) * part, :]).astype(BF16)
        rows_ref[0, m * part // 2 : (m + 1) * part // 2, :] = dealt[: part // 2]
        rows_ref[1, m * part // 2 : (m + 1) * part // 2, :] = dealt[part // 2 :]
    copies = [pltpu.make_async_copy(rows_ref, rows_hbm, out_sem.at[0])]
    copies[0].start()
    halves = ((wg_ref, wu_ref, w.at[0]), (w.at[1], w.at[2], w.at[3]))
    for h, (wg, wu, wd) in enumerate(halves):
        for load in loads[1:] if h else loads[:1]:
            load.wait()
        for lo in range(0, hid, tile):
            s = slice(lo, lo + tile)
            g = mm(wg[s, :], rows_ref[0], NT)
            u = mm(wu[s, :], rows_ref[0], NT)
            dh = mm(wd[s, :], rows_ref[1], NT)
            sig = jax.nn.sigmoid(g)
            silu = g * sig
            act[h, 0, s, :] = (silu * u).astype(BF16)
            act[h, 1, s, :] = (dh * u * sig * (1.0 + g * (1.0 - sig))).astype(BF16)
            act[h, 2, s, :] = (dh * silu).astype(BF16)
    for h, hbm in enumerate((act_hbm, act2_hbm)):
        copies.append(pltpu.make_async_copy(act.at[h], hbm, out_sem.at[1 + h]))
        copies[-1].start()
    for n in range(width // cols):
        c = slice(n * cols, (n + 1) * cols)
        p = mm(act[0, 0], w[0, :, c], TN) + mm(act[1, 0], w[3, :, c], TN)
        q = mm(act[0, 1], wg_ref[:, c], TN) + mm(act[1, 1], w[1, :, c], TN)
        q = q + mm(act[0, 2], wu_ref[:, c], TN) + mm(act[1, 2], w[2, :, c], TN)
        p, q = p.astype(BF16), q.astype(BF16)
        for m in range(rows // part):
            r = slice(m * part // 2, (m + 1) * part // 2)
            both = jnp.concatenate([p[r], q[r]], axis=0)
            sent[m * part : (m + 1) * part, c] = mm(perm, both, TN).astype(BF16)
        copies.append(pltpu.make_async_copy(sent.at[:, c], sent_hbm.at[:, c], out_sem.at[3 + n]))
        copies[-1].start()
    for copy in copies:
        copy.wait()


def expert(z, mine, theirs):
    rows, width = z.shape[0] // 2, z.shape[1]
    hid = mine[0].shape[0]
    out = lambda *n: pltpu.HBM(n, BF16)
    return pl.pallas_call(
        expert_kernel,
        in_specs=[VMEM] * 3 + [HBM] + [ANY] * 3,
        out_specs=[HBM] * 4,
        out_shape=[out(2, rows, width), out(3, hid, rows), out(3, hid, rows), out(2 * rows, width)],
        scratch_shapes=[
            pltpu.VMEM((4, hid, width), BF16),
            pltpu.VMEM((2, rows, width), BF16),
            pltpu.VMEM((2, 3, hid, rows), BF16),
            pltpu.VMEM((2 * rows, width), BF16),
            pltpu.SemaphoreType.DMA((4,)),
            pltpu.SemaphoreType.DMA((5,)),
        ],
        cost_estimate=pl.CostEstimate(
            flops=24 * rows * width * hid, bytes_accessed=12 * width * hid, transcendentals=2 * rows * hid
        ),
        compiler_params=pltpu.CompilerParams(vmem_limit_bytes=30 << 20),
        name="expert",
    )(*resident(z, *mine[:2]), pltpu.with_memory_space_constraint(mine[2], pltpu.HBM), *theirs)


def weight_grads_kernel(rows_ref, act_ref, rows2_ref, act2_ref, gg_ref, gu_ref, gd_ref):
    for i, side, out in ((0, 1, gd_ref), (1, 0, gg_ref), (2, 0, gu_ref)):
        out[...] = (mm(act_ref[i], rows_ref[side]) + mm(act2_ref[i], rows2_ref[side])).astype(BF16)


def weight_grads(rows, act, rows2, act2):
    _, count, width = rows.shape
    hid = act.shape[1]
    cols = 256
    tall = pl.BlockSpec((2, count, cols), lambda i: (0, 0, i))
    whole = pl.BlockSpec(act.shape, lambda i: (0, 0, 0))
    out = pl.BlockSpec((hid, cols), lambda i: (0, i))
    return pl.pallas_call(
        weight_grads_kernel,
        grid=(width // cols,),
        in_specs=[tall, whole, tall, whole],
        out_specs=[out] * 3,
        out_shape=[jax.ShapeDtypeStruct((hid, width), BF16)] * 3,
        cost_estimate=pl.CostEstimate(
            flops=12 * count * width * hid, bytes_accessed=6 * hid * width, transcendentals=0
        ),
        compiler_params=pltpu.CompilerParams(vmem_limit_bytes=24 << 20),
        name="weight_grads",
    )(rows, act, rows2, act2)


def select_kernel(ids_ref, gates_ref, pick_ref, choice_ref):
    ids = ids_ref[...]
    top, toks = ids.shape
    rows = choice_ref.shape[0]
    expert, is_dy, fills, gate = routing(ids, gates_ref[...], 0, rows)
    gated = jnp.where(fills & ~is_dy, gate, 0.0)
    high = gated.astype(BF16)
    low = (gated - high.astype(F32)).astype(BF16)
    pick = jnp.where(fills & is_dy, 1.0, 0.0).astype(BF16)
    for i, part in enumerate((high, low, pick)):
        pick_ref[i * toks : (i + 1) * toks, :] = part.T
    choice = jnp.full((rows, toks), -1, I32)
    for k in range(top):
        choice = jnp.where(ids[k : k + 1, :] == expert, k, choice)
    choice_ref[...] = jnp.where(fills & ~is_dy, choice, -1)


def select(ids, gates, experts):
    rows, toks = experts * 2 * CAP, ids.shape[1]
    return pl.pallas_call(
        select_kernel,
        in_specs=[VMEM] * 2,
        out_specs=[VMEM] * 2,
        out_shape=[pltpu.VMEM((3 * toks, rows), BF16), pltpu.VMEM((rows, toks), I32)],
        cost_estimate=pl.CostEstimate(flops=rows * toks * 64, bytes_accessed=rows * toks * 10, transcendentals=0),
        name="select",
    )(ids, gates)


def combine_kernel(pick_ref, choice_ref, cot_ref, back_ref, mixed_ref, dtok_ref, dgates_ref):
    toks = cot_ref.shape[0]
    back = back_ref[...]
    sums = mm(pick_ref[...], back)
    mixed_ref[...] = (sums[:toks] + sums[toks : 2 * toks]).astype(BF16)
    dtok_ref[...] = sums[2 * toks :].astype(BF16)
    inner = mm(back, cot_ref[...], NT)
    choice = choice_ref[...]
    for k in range(dgates_ref.shape[0]):
        dgates_ref[k : k + 1, :] = jnp.sum(jnp.where(choice == k, inner, 0.0), axis=0, keepdims=True)


def combine(pick, choice, cot, back, top):
    return pl.pallas_call(
        combine_kernel,
        in_specs=[VMEM] * 4,
        out_specs=[VMEM] * 3,
        out_shape=[
            jax.ShapeDtypeStruct(cot.shape, BF16),
            jax.ShapeDtypeStruct(cot.shape, BF16),
            jax.ShapeDtypeStruct((top, cot.shape[0]), F32),
        ],
        compiler_params=pltpu.CompilerParams(vmem_limit_bytes=32 << 20),
        name="combine",
    )(*resident(pick, choice, cot, back))


def route(rows):
    chips = lax.axis_size(("expert", "chip"))
    width = rows.shape[1]
    blocks = rows.reshape(chips, -1, width)
    return lax.all_to_all(blocks, ("expert", "chip"), 0, 0, tiled=True).reshape(-1, width)


def swap(rows):
    return lax.ppermute(rows, "core", [(0, 1), (1, 0)])


def local(tokens, expert_ids, gate_weights, cotangent, w_gate, w_up, w_down):
    ids, gates = expert_ids.T, gate_weights.T
    experts = lax.axis_size(("expert", "chip"))
    mine = (w_gate[0].T, w_up[0].T, w_down[0])
    theirs = tuple(swap(w) for w in mine)
    z = route(pack(ids, gates, tokens, cotangent, experts))
    rows, act, act_theirs, sent = expert(z, mine, theirs)
    rows2, act2 = swap(rows), swap(act_theirs)
    back = route(sent)
    ids, gates, _ = lax.optimization_barrier((ids, gates, sent[:8, :128]))
    pick, choice = select(ids, gates, experts)
    grads = weight_grads(rows, act, rows2, act2)
    pick, choice, grad_gate, grad_up, grad_down = lax.optimization_barrier((pick, choice, *grads))
    mixed, d_tokens, d_gates = combine(pick, choice, cotangent, back, ids.shape[0])
    return (mixed, d_tokens, d_gates.T, grad_gate.T[None], grad_up.T[None], grad_down[None])


def solution(mesh):
    outer, inner = mesh.devices.shape
    chips = Mesh(mesh.devices.reshape(outer, inner // 2, 2), ("expert", "chip", "core"))
    split = ("expert", "chip", "core")
    flat, tall = P(split, None), P(split, None, None)
    return jax.shard_map(
        local,
        mesh=chips,
        in_specs=(flat, flat, flat, flat, tall, tall, tall),
        out_specs=(flat, flat, flat, tall, tall, tall),
        check_vma=False,
    )
```

time: 112 us -> 103 us (0.920)
  local copies, waits for them, and re-layouts: 12.7 us -> 2.85 us
  other arithmetic: 2.27 us -> 0 us
  Pallas kernels: 30.2 us -> 32.1 us
    unnamed x48 -> x12, local copies, waits for them, and re-layouts: 12.7 us -> 2.85 us
    ppermute x2 -> x5, waiting for transfers between devices: 3.79 us -> 1.42 us  [swap(): return lax.ppermute(rows, 'core', [(0, 1), (1, 0)])]
    reshape x1 -> x0, other arithmetic: 2.27 us -> none  [route(): blocks = rows.reshape(chips, -1, width)]
    pallas_call x4 -> x2, Pallas kernels: 14.1 us -> 16.2 us  [the longest x1 15 us: expert(): pl.pallas_call(expert_kernel, in_specs=[VMEM] * 3 + [HBM] + [ANY] * 3, ou...]
    all_to_all x1, waiting for transfers between devices: 12.9 us -> 14.8 us  [route(): lax.all_to_all(blocks, ('expert', 'chip'), 0, 0, tiled=True)]
    pallas_call x1, Pallas kernels: 8.65 us -> 9.87 us  [weight_grads(): pl.pallas_call(weight_grads_kernel, grid=(width // cols,), in_specs=[tall...]
    pallas_call x1, Pallas kernels: 2.87 us -> 1.69 us  [combine(): pl.pallas_call(combine_kernel, in_specs=[VMEM] * 4, out_specs=[VMEM] * 3,...]
    ppermute x2 -> x5, starting transfers between devices: 3.53 us -> 3.88 us  [swap(): return lax.ppermute(rows, 'core', [(0, 1), (1, 0)])]
  transfers between devices with their start and end apart: 3 -> 6, of which waited for: 2 -> 2; matrix products, arithmetic and copies ran while one was open for 0% -> 0% of each run, Pallas kernels for 14% -> 15%
where the time goes in v1:
time: 103 us; the launch traced here: 102 us
  blocking collectives  41.7 us (40%)
  Pallas kernels  32.1 us (31%)
  waiting for transfers between devices  16.2 us (16%)
  starting transfers between devices  8.75 us (8%)
  local copies, waits for them, and re-layouts  2.85 us (3%)
    all_to_all x1, blocking collectives, route(): lax.all_to_all(blocks, ('expert', 'chip'), 0, 0, tiled=True)  41.7 us
    pallas_call x1, Pallas kernels, expert(): pl.pallas_call(expert_kernel, in_specs=[VMEM] * 3 + [HBM] + [ANY] * 3, ou...  15 us
    all_to_all x1, waiting for transfers between devices, route(): lax.all_to_all(blocks, ('expert', 'chip'), 0, 0, tiled=True)  14.8 us
    pallas_call x1, Pallas kernels, weight_grads(): pl.pallas_call(weight_grads_kernel, grid=(width // cols,), in_specs=[tall...  9.87 us
    all_to_all x1, starting transfers between devices, route(): lax.all_to_all(blocks, ('expert', 'chip'), 0, 0, tiled=True)  4.87 us
    pallas_call x1, Pallas kernels, pack(): pl.pallas_call(pack_kernel, grid=(steps,), in_specs=[whole(ids), whole(ga...  4.33 us
    ppermute x5, starting transfers between devices, swap(): return lax.ppermute(rows, 'core', [(0, 1), (1, 0)])  3.88 us
    unnamed x12, local copies, waits for them, and re-layouts  2.85 us
  transfers between devices with their start and end apart: 6, of which 2 were waited for; matrix products, arithmetic and copies ran while one was open for 0% of the time, Pallas kernels for 15%

profile of v1, /device:TPU:1, one launch (start us, length us, event | category | flops | bytes accessed | tf_op | source)
XLA Modules:
  0.0 102.3 jit_solution(2208763671383855843)
XLA Ops:
  0.6 1.5 %collective-permute-start = (bf16[704,2048]{1,0:T(8,128)(2,1)}, bf16[704,2048]{1,0:T(8,128)(2,1)}, u32[]{:S(2)}, u32[]{:S(2)}) collective-permute-start(bf16[704,2048]{1,0:T(8,128)(2,1)} %bitcast.23), channel_id=1, source_target_pairs={{0,1},{1,0},{2,3},{3,2},{4,5},{5,4},{6,7},{7,6},{8,9},{9,8},{10,11... | collective-permute-start | bytes 8650760 | tf_op jit(solution)/shard_map/ppermute | solution.py:243
  2.1 0.1 collective-permute-start.1
  2.2 0.4 collective-permute-start.2
  2.6 0.0 copy-start.1
  2.6 4.3 %pack.1 = bf16[512,2048]{1,0:T(8,128)(2,1)} custom-call(s32[6,32]{1,0:T(8,128)} %bitcast.29, f32[6,32]{1,0:T(8,128)} %bitcast.31, bf16[32,2048]{1,0:T(8,128)(2,1)} %tok_ref.1, bf16[32,2048]{1,0:T(8,128)(2,1)} %cot_ref.3), custom_call_target="tpu_custom_call" | custom-call | tf_op jit(solution)/shard_map/pack/pallas_call | solution.py:58
  7.0 0.0 copy-start.2
  7.0 41.7 %all_to_all.10 = bf16[64,8,2048]{2,1,0:T(8,128)(2,1)S(1)} all-to-all(bf16[64,8,2048]{2,1,0:T(8,128)(2,1)} %bitcast.27), channel_id=1, replica_groups=mesh['expert'=4,'chip'=16,'core'=2] {'expert','chip'}, dimensions={0} | all-to-all | bytes 4194304 | tf_op jit(solution)/shard_map/all_to_all | solution.py:239
  48.6 0.0 collective-permute-done.wg2_hbm
  48.7 0.0 collective-permute-done.1.wu2_hbm
  48.7 0.0 collective-permute-done.2.wd2_hbm
  48.7 0.0 copy-done.1
  48.7 0.0 copy-done.2
  48.7 15.0 %expert.1 = (bf16[2,256,2048]{2,1,0:T(8,128)(2,1)}, bf16[3,704,256]{2,1,0:T(8,128)(2,1)}, bf16[3,704,256]{2,1,0:T(8,128)(2,1)}, bf16[512,2048]{1,0:T(8,128)(2,1)}) custom-call(bf16[512,2048]{1,0:T(8,128)(2,1)S(1)} %bitcast.22, bf16[704,2048]{1,0:T(8,128)(2,1)S(1)} %bitcast.24, bf16[704,2048]{1,0:T(8,128)(2,1)S(1)} %bitcast.26, bf16[704,2048]{1,0:T(8,128)(2,1)} %bitcast.34, ...), custom_call_target="tpu_custom_call" | custom-call | flops 8858370048 | bytes 17301504 | tf_op jit(solution)/shard_map/expert/pallas_call | solution.py:132
  63.6 0.0 copy-start.5
  63.7 1.6 %collective-permute-start.3 = (bf16[2,256,2048]{2,1,0:T(8,128)(2,1)}, bf16[2,256,2048]{2,1,0:T(8,128)(2,1)}, u32[]{:S(2)}, u32[]{:S(2)}) collective-permute-start(bf16[2,256,2048]{2,1,0:T(8,128)(2,1)} %get-tuple-element.29.rows_ref), channel_id=1, source_target_pairs={{0,1},{1,0},{2,3},{3,2},{4,5},{5,4},{6,7},{7,6},{8,9},{9,8},{10,11... | collective-permute-start | bytes 6291464 | tf_op jit(solution)/shard_map/ppermute | solution.py:243
  65.3 4.9 %all-to-all-start.1 = ((bf16[64,8,2048]{2,1,0:T(8,128)(2,1)}), bf16[64,8,2048]{2,1,0:T(8,128)(2,1)S(1)}, u32[]{:S(2)}, u32[]{:S(2)}) async-start(bf16[64,8,2048]{2,1,0:T(8,128)(2,1)} %bitcast.28), calls=%async_computation.1 | async-start | bytes 4194304 | tf_op jit(solution)/shard_map/all_to_all | solution.py:239
  70.2 0.0 copy-done.5
  70.2 0.2 collective-permute-start.4
  70.4 1.3 %select.1 = (bf16[96,512]{1,0:T(8,128)(2,1)S(1)}, s32[512,32]{1,0:T(8,128)S(1)}) custom-call(s32[6,32]{1,0:T(8,128)} %bitcast.30, f32[6,32]{1,0:T(8,128)} %bitcast.32), custom_call_target="tpu_custom_call" | custom-call | flops 1048576 | bytes 163840 | tf_op jit(solution)/shard_map/select/pallas_call | solution.py:198
  71.7 1.4 %collective-permute-done.4.act2_ref = bf16[3,704,256]{2,1,0:T(8,128)(2,1)} collective-permute-done((bf16[3,704,256]{2,1,0:T(8,128)(2,1)S(1)}, bf16[3,704,256]{2,1,0:T(8,128)(2,1)}, u32[]{:S(2)}, u32[]{:S(2)}) %collective-permute-start.4) | collective-permute-done | bytes 1081376 | tf_op jit(solution)/shard_map/ppermute | solution.py:243
  73.1 0.0 collective-permute-done.3.rows2_ref
  73.1 0.0 copy-start.3
  73.1 1.6 %copy-done.3 = bf16[2,256,2048]{2,1,0:T(8,128)(2,1)S(1)} copy-done((bf16[2,256,2048]{2,1,0:T(8,128)(2,1)S(1)}, bf16[2,256,2048]{2,1,0:T(8,128)(2,1)}, u32[]{:S(2)}) %copy-start.3) | copy-done | bytes 2097176
  74.7 0.0 copy-start.4
  74.7 1.2 %copy-done.4 = bf16[3,704,256]{2,1,0:T(8,128)(2,1)S(1)} copy-done((bf16[3,704,256]{2,1,0:T(8,128)(2,1)S(1)}, bf16[3,704,256]{2,1,0:T(8,128)(2,1)}, u32[]{:S(2)}) %copy-start.4) | copy-done | bytes 1081368
  75.9 0.0 copy-start
  75.9 9.9 %weight_grads.1 = (bf16[704,2048]{1,0:T(8,128)(2,1)}, bf16[704,2048]{1,0:T(8,128)(2,1)}, bf16[704,2048]{1,0:T(8,128)(2,1)}) custom-call(bf16[2,256,2048]{2,1,0:T(8,128)(2,1)S(1)} %copy-done.3, bf16[3,704,256]{2,1,0:T(8,128)(2,1)S(1)} %copy-done.4, bf16[2,256,2048]{2,1,0:T(8,128)(2,1)} %collective-permute-done.3.rows2_ref, ...), custom_call_target="tpu_custom_call" | custom-call | flops 4429185024 | bytes 8650752 | tf_op jit(solution)/shard_map/weight_grads/pallas_call | solution.py:165
  85.8 14.8 %all-to-all-done.1 = bf16[64,8,2048]{2,1,0:T(8,128)(2,1)S(1)} async-done(((bf16[64,8,2048]{2,1,0:T(8,128)(2,1)}), bf16[64,8,2048]{2,1,0:T(8,128)(2,1)S(1)}, u32[]{:S(2)}, u32[]{:S(2)}) %all-to-all-start.1) | async-done | bytes 2097184 | tf_op jit(solution)/shard_map/all_to_all | solution.py:239
  100.6 0.0 copy-done
  100.6 1.7 %combine.1 = (bf16[32,2048]{1,0:T(8,128)(2,1)}, bf16[32,2048]{1,0:T(8,128)(2,1)}, f32[6,32]{1,0:T(8,128)}) custom-call(bf16[96,512]{1,0:T(8,128)(2,1)S(1)} %get-tuple-element.35.pick_ref, s32[512,32]{1,0:T(8,128)S(1)} %get-tuple-element.36.choice_ref, bf16[32,2048]{1,0:T(8,128)(2,1)S(1)} %copy-done, bf16[512,2048]{1,0:T(8,128)(2,1)S(1)} %bitcast.21), custom_call_target="tpu_custom_call" | custom-call | tf_op jit(solution)/shard_map/combine/pallas_call | solution.py:221
Async XLA Ops:
  0.6 48.0 %collective-permute-start = (bf16[704,2048]{1,0:T(8,128)(2,1)}, bf16[704,2048]{1,0:T(8,128)(2,1)}, u32[]{:S(2)}, u32[]{:S(2)}) collective-permute-start(bf16[704,2048]{1,0:T(8,128)(2,1)} %bitcast.23), channel_id=1, source_target_pairs={{0,1},{1,0},{2,3},{3,2},{4,5},{5,4},{6,7},{7,6},{8,9},{9,8},{10,11... | collective-permute-start | bytes 8650760 | tf_op jit(solution)/shard_map/ppermute | solution.py:243
  2.1 46.5 %collective-permute-start.1 = (bf16[704,2048]{1,0:T(8,128)(2,1)}, bf16[704,2048]{1,0:T(8,128)(2,1)}, u32[]{:S(2)}, u32[]{:S(2)}) collective-permute-start(bf16[704,2048]{1,0:T(8,128)(2,1)} %bitcast.25), channel_id=1, source_target_pairs={{0,1},{1,0},{2,3},{3,2},{4,5},{5,4},{6,7},{7,6},{8,9},{9,8},{10,11... | collective-permute-start | bytes 8650760 | tf_op jit(solution)/shard_map/ppermute | solution.py:243
  2.2 46.4 %collective-permute-start.2 = (bf16[704,2048]{1,0:T(8,128)(2,1)}, bf16[704,2048]{1,0:T(8,128)(2,1)}, u32[]{:S(2)}, u32[]{:S(2)}) collective-permute-start(bf16[704,2048]{1,0:T(8,128)(2,1)} %bitcast.33), channel_id=1, source_target_pairs={{0,1},{1,0},{2,3},{3,2},{4,5},{5,4},{6,7},{7,6},{8,9},{9,8},{10,11... | collective-permute-start | bytes 8650760 | tf_op jit(solution)/shard_map/ppermute | solution.py:243
  2.6 46.0 %copy-start.1 = (bf16[1,2048,704]{1,2,0:T(8,128)(2,1)S(1)}, bf16[1,2048,704]{1,2,0:T(8,128)(2,1)}, u32[]{:S(2)}) copy-start(bf16[1,2048,704]{1,2,0:T(8,128)(2,1)} %param.11) | copy-start | bytes 8650756
  7.0 41.7 %copy-start.2 = (bf16[1,2048,704]{1,2,0:T(8,128)(2,1)S(1)}, bf16[1,2048,704]{1,2,0:T(8,128)(2,1)}, u32[]{:S(2)}) copy-start(bf16[1,2048,704]{1,2,0:T(8,128)(2,1)} %param.12) | copy-start | bytes 8650756
  63.6 6.5 %copy-start.5 = (bf16[3,704,256]{2,1,0:T(8,128)(2,1)S(1)}, bf16[3,704,256]{2,1,0:T(8,128)(2,1)}, u32[]{:S(2)}) copy-start(bf16[3,704,256]{2,1,0:T(8,128)(2,1)} %get-tuple-element.31) | copy-start | bytes 3244036
  63.7 9.4 %collective-permute-start.3 = (bf16[2,256,2048]{2,1,0:T(8,128)(2,1)}, bf16[2,256,2048]{2,1,0:T(8,128)(2,1)}, u32[]{:S(2)}, u32[]{:S(2)}) collective-permute-start(bf16[2,256,2048]{2,1,0:T(8,128)(2,1)} %get-tuple-element.29.rows_ref), channel_id=1, source_target_pairs={{0,1},{1,0},{2,3},{3,2},{4,5},{5,4},{6,7},{7,6},{8,9},{9,8},{10,11... | collective-permute-start | bytes 6291464 | tf_op jit(solution)/shard_map/ppermute | solution.py:243
  65.3 35.3 %all-to-all-start.1 = ((bf16[64,8,2048]{2,1,0:T(8,128)(2,1)}), bf16[64,8,2048]{2,1,0:T(8,128)(2,1)S(1)}, u32[]{:S(2)}, u32[]{:S(2)}) async-start(bf16[64,8,2048]{2,1,0:T(8,128)(2,1)} %bitcast.28), calls=%async_computation.1 | async-start | bytes 4194304 | tf_op jit(solution)/shard_map/all_to_all | solution.py:239
  70.2 2.9 %collective-permute-start.4 = (bf16[3,704,256]{2,1,0:T(8,128)(2,1)S(1)}, bf16[3,704,256]{2,1,0:T(8,128)(2,1)}, u32[]{:S(2)}, u32[]{:S(2)}) collective-permute-start(bf16[3,704,256]{2,1,0:T(8,128)(2,1)S(1)} %copy-done.5), channel_id=1, source_target_pairs={{0,1},{1,0},{2,3},{3,2},{4,5},{5,4},{6,7},{7,6},{8,9},{9,8},{10,11... | collective-permute-start | bytes 3244040 | tf_op jit(solution)/shard_map/ppermute | solution.py:243
  73.1 1.6 %copy-start.3 = (bf16[2,256,2048]{2,1,0:T(8,128)(2,1)S(1)}, bf16[2,256,2048]{2,1,0:T(8,128)(2,1)}, u32[]{:S(2)}) copy-start(bf16[2,256,2048]{2,1,0:T(8,128)(2,1)} %get-tuple-element.29.rows_ref) | copy-start | bytes 6291460
  74.7 1.2 %copy-start.4 = (bf16[3,704,256]{2,1,0:T(8,128)(2,1)S(1)}, bf16[3,704,256]{2,1,0:T(8,128)(2,1)}, u32[]{:S(2)}) copy-start(bf16[3,704,256]{2,1,0:T(8,128)(2,1)} %get-tuple-element.30.act_ref) | copy-start | bytes 3244036
  75.9 24.6 %copy-start = (bf16[32,2048]{1,0:T(8,128)(2,1)S(1)}, bf16[32,2048]{1,0:T(8,128)(2,1)}, u32[]{:S(2)}) copy-start(bf16[32,2048]{1,0:T(8,128)(2,1)} %cot_ref.3) | copy-start | bytes 393220

commit v2 on v1

--- a/solution.py
+++ b/solution.py
@@ -40,29 +40,60 @@
     return expert, is_dy, fills, gate
 
 
-def pack_kernel(ids_ref, gates_ref, tok_ref, cot_ref, out_ref):
-    rows = out_ref.shape[0]
-    _, is_dy, fills, gate = routing(ids_ref[...], gates_ref[...], pl.program_id(0) * rows, rows)
-    pick_x = jnp.where(fills & ~is_dy, 1.0, 0.0)
-    pick_dy = jnp.where(fills & is_dy, 1.0, 0.0)
-    scale = jnp.sum(pick_x + pick_dy * gate, axis=1, keepdims=True)
-    pick = jnp.concatenate([pick_x, pick_dy], axis=1).astype(BF16)
-    both = jnp.concatenate([tok_ref[...], cot_ref[...]], axis=0)
-    out_ref[...] = (mm(pick, both) * scale).astype(BF16)
-
-
-def pack(ids, gates, tokens, cot, experts):
-    rows, steps = experts * 2 * CAP, 4
-    width = tokens.shape[1]
-    whole = lambda a: pl.BlockSpec(a.shape, lambda i: (0, 0))
+def pack_kernel(ids_hbm, gates_hbm, tok_hbm, cot_hbm, w_hbm, out_hbm, w_ref, *refs):
+    ids_ref, gates_ref, both_ref, packed, in_sem, out_sem = refs
+    steps = out_sem.shape[0]
+    rows, toks = packed.shape[0] // steps, tok_hbm.shape[0]
+    pairs = (
+        (ids_hbm, ids_ref),
+        (gates_hbm, gates_ref),
+        (tok_hbm, both_ref.at[:toks]),
+        (cot_hbm, both_ref.at[toks:]),
+        (w_hbm, w_ref),
+    )
+    loads = [pltpu.make_async_copy(source, target, in_sem.at[i]) for i, (source, target) in enumerate(pairs)]
+    for load in loads:
+        load.start()
+    for load in loads[:4]:
+        load.wait()
+    both = both_ref[...]
+    copies = []
+    for i in range(steps):
+        _, is_dy, fills, gate = routing(ids_ref[...], gates_ref[...], i * rows, rows)
+        pick_x = jnp.where(fills & ~is_dy, 1.0, 0.0)
+        pick_dy = jnp.where(fills & is_dy, 1.0, 0.0)
+        scale = jnp.sum(pick_x + pick_dy * gate, axis=1, keepdims=True)
+        pick = jnp.concatenate([pick_x, pick_dy], axis=1).astype(BF16)
+        s = slice(i * rows, (i + 1) * rows)
+        packed[s, :] = (mm(pick, both) * scale).astype(BF16)
+        copies.append(pltpu.make_async_copy(packed.at[s], out_hbm.at[s], out_sem.at[i]))
+        copies[-1].start()
+    for copy in copies:
+        copy.wait()
+    loads[4].wait()
+
+
+def pack(ids, gates, tokens, cot, weight, experts):
+    rows, width = experts * 2 * CAP, tokens.shape[1]
     return pl.pallas_call(
         pack_kernel,
-        grid=(steps,),
-        in_specs=[whole(ids), whole(gates), whole(tokens), whole(cot)],
-        out_specs=pl.BlockSpec((rows // steps, width), lambda i: (i, 0)),
-        out_shape=jax.ShapeDtypeStruct((rows, width), BF16),
+        in_specs=[HBM] * 5,
+        out_specs=[HBM, VMEM],
+        out_shape=[pltpu.HBM((rows, width), BF16), pltpu.VMEM(weight.shape, BF16)],
+        scratch_shapes=[
+            pltpu.VMEM(ids.shape, I32),
+            pltpu.VMEM(gates.shape, F32),
+            pltpu.VMEM((2 * tokens.shape[0], width), BF16),
+            pltpu.VMEM((rows, width), BF16),
+            pltpu.SemaphoreType.DMA((5,)),
+            pltpu.SemaphoreType.DMA((4,)),
+        ],
+        cost_estimate=pl.CostEstimate(
+            flops=4 * rows * width * ids.shape[1], bytes_accessed=2 * rows * width, transcendentals=0
+        ),
+        compiler_params=pltpu.CompilerParams(vmem_limit_bytes=12 << 20),
         name="pack",
-    )(ids, gates, tokens, cot)
+    )(*(pltpu.with_memory_space_constraint(a, pltpu.HBM) for a in (ids, gates, tokens, cot, weight)))
 
 
 def deal(size):
@@ -74,53 +105,47 @@
     return jnp.where(source == q, 1.0, 0.0).astype(BF16)
 
 
-def expert_kernel(z_ref, wg_ref, wu_ref, wd_hbm, wg2_hbm, wu2_hbm, wd2_hbm, *refs):
-    rows_hbm, act_hbm, act2_hbm, sent_hbm = refs[:4]
-    w, rows_ref, act, sent, w_sem, out_sem = refs[4:]
-    part, tile, cols = 256, 352, 1024
+def expert_kernel(z_ref, wg, wu, wd, wg2, wu2, wd2, rows_hbm, act_hbm, act2_hbm, sent_hbm, *refs):
+    rows_ref, act, sent, out_sem = refs
+    part, tile, cols = 256, 352, 512
     rows, width = z_ref.shape
-    hid = wg_ref.shape[0]
-    loads = [
-        pltpu.make_async_copy(hbm, w.at[i], w_sem.at[i]) for i, hbm in enumerate((wd_hbm, wg2_hbm, wu2_hbm, wd2_hbm))
-    ]
-    for load in loads:
-        load.start()
+    hid = wg.shape[0]
     perm = deal(part)
     for m in range(rows // part):
         dealt = mm(perm, z_ref[m * part : (m + 1) * part, :]).astype(BF16)
         rows_ref[0, m * part // 2 : (m + 1) * part // 2, :] = dealt[: part // 2]
         rows_ref[1, m * part // 2 : (m + 1) * part // 2, :] = dealt[part // 2 :]
-    copies = [pltpu.make_async_copy(rows_ref, rows_hbm, out_sem.at[0])]
-    copies[0].start()
-    halves = ((wg_ref, wu_ref, w.at[0]), (w.at[1], w.at[2], w.at[3]))
-    for h, (wg, wu, wd) in enumerate(halves):
-        for load in loads[1:] if h else loads[:1]:
-            load.wait()
+    copies = []
+
+    def send(source, target):
+        copies.append(pltpu.make_async_copy(source, target, out_sem.at[len(copies)]))
+        copies[-1].start()
+
+    send(rows_ref, rows_hbm)
+    for h, (wg_h, wu_h, wd_h) in enumerate(((wg, wu, wd), (wg2, wu2, wd2))):
         for lo in range(0, hid, tile):
             s = slice(lo, lo + tile)
-            g = mm(wg[s, :], rows_ref[0], NT)
-            u = mm(wu[s, :], rows_ref[0], NT)
-            dh = mm(wd[s, :], rows_ref[1], NT)
+            g = mm(wg_h[s, :], rows_ref[0], NT)
+            u = mm(wu_h[s, :], rows_ref[0], NT)
+            dh = mm(wd_h[s, :], rows_ref[1], NT)
             sig = jax.nn.sigmoid(g)
             silu = g * sig
             act[h, 0, s, :] = (silu * u).astype(BF16)
-            act[h, 1, s, :] = (dh * u * sig * (1.0 + g * (1.0 - sig))).astype(BF16)
+            act[h, 1, s, :] = (dh * u * (sig + silu * (1.0 - sig))).astype(BF16)
             act[h, 2, s, :] = (dh * silu).astype(BF16)
-    for h, hbm in enumerate((act_hbm, act2_hbm)):
-        copies.append(pltpu.make_async_copy(act.at[h], hbm, out_sem.at[1 + h]))
-        copies[-1].start()
+    send(act.at[0], act_hbm)
+    send(act.at[1], act2_hbm)
     for n in range(width // cols):
         c = slice(n * cols, (n + 1) * cols)
-        p = mm(act[0, 0], w[0, :, c], TN) + mm(act[1, 0], w[3, :, c], TN)
-        q = mm(act[0, 1], wg_ref[:, c], TN) + mm(act[1, 1], w[1, :, c], TN)
-        q = q + mm(act[0, 2], wu_ref[:, c], TN) + mm(act[1, 2], w[2, :, c], TN)
+        p = mm(act[0, 0], wd[:, c], TN) + mm(act[1, 0], wd2[:, c], TN)
+        q = mm(act[0, 1], wg[:, c], TN) + mm(act[1, 1], wg2[:, c], TN)
+        q = q + mm(act[0, 2], wu[:, c], TN) + mm(act[1, 2], wu2[:, c], TN)
         p, q = p.astype(BF16), q.astype(BF16)
         for m in range(rows // part):
             r = slice(m * part // 2, (m + 1) * part // 2)
             both = jnp.concatenate([p[r], q[r]], axis=0)
             sent[m * part : (m + 1) * part, c] = mm(perm, both, TN).astype(BF16)
-        copies.append(pltpu.make_async_copy(sent.at[:, c], sent_hbm.at[:, c], out_sem.at[3 + n]))
-        copies[-1].start()
+        send(sent.at[:, c], sent_hbm.at[:, c])
     for copy in copies:
         copy.wait()
 
@@ -131,23 +156,21 @@
     out = lambda *n: pltpu.HBM(n, BF16)
     return pl.pallas_call(
         expert_kernel,
-        in_specs=[VMEM] * 3 + [HBM] + [ANY] * 3,
+        in_specs=[VMEM] * 7,
         out_specs=[HBM] * 4,
         out_shape=[out(2, rows, width), out(3, hid, rows), out(3, hid, rows), out(2 * rows, width)],
         scratch_shapes=[
-            pltpu.VMEM((4, hid, width), BF16),
             pltpu.VMEM((2, rows, width), BF16),
             pltpu.VMEM((2, 3, hid, rows), BF16),
             pltpu.VMEM((2 * rows, width), BF16),
-            pltpu.SemaphoreType.DMA((4,)),
-            pltpu.SemaphoreType.DMA((5,)),
+            pltpu.SemaphoreType.DMA((7,)),
         ],
         cost_estimate=pl.CostEstimate(
             flops=24 * rows * width * hid, bytes_accessed=12 * width * hid, transcendentals=2 * rows * hid
         ),
-        compiler_params=pltpu.CompilerParams(vmem_limit_bytes=30 << 20),
+        compiler_params=pltpu.CompilerParams(vmem_limit_bytes=20 << 20),
         name="expert",
-    )(*resident(z, *mine[:2]), pltpu.with_memory_space_constraint(mine[2], pltpu.HBM), *theirs)
+    )(*resident(z, *mine, *theirs))
 
 
 def weight_grads_kernel(rows_ref, act_ref, rows2_ref, act2_ref, gg_ref, gu_ref, gd_ref):
@@ -248,8 +271,9 @@
     experts = lax.axis_size(("expert", "chip"))
     mine = (w_gate[0].T, w_up[0].T, w_down[0])
     theirs = tuple(swap(w) for w in mine)
-    z = route(pack(ids, gates, tokens, cotangent, experts))
-    rows, act, act_theirs, sent = expert(z, mine, theirs)
+    packed, down = pack(ids, gates, tokens, cotangent, mine[2], experts)
+    z = route(packed)
+    rows, act, act_theirs, sent = expert(z, (*mine[:2], down), theirs)
     rows2, act2 = swap(rows), swap(act_theirs)
     back = route(sent)
     ids, gates, _ = lax.optimization_barrier((ids, gates, sent[:8, :128]))

time: 103 us -> 99.8 us (0.969)
  Pallas kernels: 32.1 us -> 29.1 us
    pallas_call x2, Pallas kernels: 19.3 us -> 16.3 us  [the longest x1 12.3 us: expert(): pl.pallas_call(expert_kernel, in_specs=[VMEM] * 7, out_specs=[HBM] * 4, o...]
where the time goes in v2:
time: 99.8 us; the launch traced here: 99.1 us
  blocking collectives  41.7 us (42%)
  Pallas kernels  29.1 us (29%)
  waiting for transfers between devices  16.2 us (16%)
  starting transfers between devices  8.57 us (9%)
  local copies, waits for them, and re-layouts  2.85 us (3%)
    all_to_all x1, blocking collectives, route(): lax.all_to_all(blocks, ('expert', 'chip'), 0, 0, tiled=True)  41.7 us
    all_to_all x1, waiting for transfers between devices, route(): lax.all_to_all(blocks, ('expert', 'chip'), 0, 0, tiled=True)  14.8 us
    pallas_call x1, Pallas kernels, expert(): pl.pallas_call(expert_kernel, in_specs=[VMEM] * 7, out_specs=[HBM] * 4, o...  12.3 us
    pallas_call x1, Pallas kernels, weight_grads(): pl.pallas_call(weight_grads_kernel, grid=(width // cols,), in_specs=[tall...  9.88 us
    all_to_all x1, starting transfers between devices, route(): lax.all_to_all(blocks, ('expert', 'chip'), 0, 0, tiled=True)  4.69 us
    pallas_call x1, Pallas kernels, pack(): pl.pallas_call(pack_kernel, in_specs=[HBM] * 5, out_specs=[HBM, VMEM], ou...  3.99 us
    ppermute x5, starting transfers between devices, swap(): return lax.ppermute(rows, 'core', [(0, 1), (1, 0)])  3.88 us
    unnamed x12, local copies, waits for them, and re-layouts  2.85 us
  transfers between devices with their start and end apart: 6, of which 2 were waited for; matrix products, arithmetic and copies ran while one was open for 0% of the time, Pallas kernels for 15%

profile of v2, /device:TPU:1, one launch (start us, length us, event | category | flops | bytes accessed | tf_op | source)
XLA Modules:
  0.0 99.1 jit_solution(4935082660773877350)
XLA Ops:
  0.6 1.5 %collective-permute-start = (bf16[704,2048]{1,0:T(8,128)(2,1)}, bf16[704,2048]{1,0:T(8,128)(2,1)S(1)}, u32[]{:S(2)}, u32[]{:S(2)}) collective-permute-start(bf16[704,2048]{1,0:T(8,128)(2,1)} %bitcast.23), channel_id=1, source_target_pairs={{0,1},{1,0},{2,3},{3,2},{4,5},{5,4},{6,7},{7,6},{8,9},{9,8},{10,11... | collective-permute-start | bytes 8650760 | tf_op jit(solution)/shard_map/ppermute | solution.py:266
  2.1 0.1 collective-permute-start.1
  2.2 0.4 collective-permute-start.2
  2.6 0.0 copy-start.2
  2.6 4.0 %pack.1 = (bf16[512,2048]{1,0:T(8,128)(2,1)}, bf16[704,2048]{1,0:T(8,128)(2,1)S(1)}) custom-call(s32[6,32]{1,0:T(8,128)} %bitcast.31, f32[6,32]{1,0:T(8,128)} %bitcast.33, bf16[32,2048]{1,0:T(8,128)(2,1)} %tok_hbm.1, bf16[32,2048]{1,0:T(8,128)(2,1)} %cot_ref.1, bf16[704,2048]{1,0:T(8,128)(2,1)} %bitcast.28), custom_call_target="tpu_custom_call" | custom-call | flops 134217728 | bytes 2097152 | tf_op jit(solution)/shard_map/pack/pallas_call | solution.py:78
  6.6 0.0 copy-start.1
  6.7 41.7 %all_to_all.10 = bf16[64,8,2048]{2,1,0:T(8,128)(2,1)S(1)} all-to-all(bf16[64,8,2048]{2,1,0:T(8,128)(2,1)} %bitcast.30), channel_id=1, replica_groups=mesh['expert'=4,'chip'=16,'core'=2] {'expert','chip'}, dimensions={0} | all-to-all | bytes 4194304 | tf_op jit(solution)/shard_map/all_to_all | solution.py:262
  48.4 0.0 collective-permute-done.wg2
  48.4 0.0 collective-permute-done.1.wu2
  48.4 0.0 collective-permute-done.2.wd2
  48.4 0.0 copy-done.2
  48.4 0.0 copy-done.1
  48.4 12.3 %expert.1 = (bf16[2,256,2048]{2,1,0:T(8,128)(2,1)}, bf16[3,704,256]{2,1,0:T(8,128)(2,1)}, bf16[3,704,256]{2,1,0:T(8,128)(2,1)}, bf16[512,2048]{1,0:T(8,128)(2,1)}) custom-call(bf16[512,2048]{1,0:T(8,128)(2,1)S(1)} %bitcast.22, bf16[704,2048]{1,0:T(8,128)(2,1)S(1)} %bitcast.24, bf16[704,2048]{1,0:T(8,128)(2,1)S(1)} %bitcast.26, ...), custom_call_target="tpu_custom_call" | custom-call | flops 8858370048 | bytes 17301504 | tf_op jit(solution)/shard_map/expert/pallas_call | solution.py:157
  60.7 0.0 copy-start.5
  60.7 1.6 %collective-permute-start.3 = (bf16[2,256,2048]{2,1,0:T(8,128)(2,1)}, bf16[2,256,2048]{2,1,0:T(8,128)(2,1)}, u32[]{:S(2)}, u32[]{:S(2)}) collective-permute-start(bf16[2,256,2048]{2,1,0:T(8,128)(2,1)} %get-tuple-element.33.rows_ref), channel_id=1, source_target_pairs={{0,1},{1,0},{2,3},{3,2},{4,5},{5,4},{6,7},{7,6},{8,9},{9,8},{10,11... | collective-permute-start | bytes 6291464 | tf_op jit(solution)/shard_map/ppermute | solution.py:266
  62.4 4.7 %all-to-all-start.1 = ((bf16[64,8,2048]{2,1,0:T(8,128)(2,1)}), bf16[64,8,2048]{2,1,0:T(8,128)(2,1)S(1)}, u32[]{:S(2)}, u32[]{:S(2)}) async-start(bf16[64,8,2048]{2,1,0:T(8,128)(2,1)} %bitcast.29), calls=%async_computation.1 | async-start | bytes 4194304 | tf_op jit(solution)/shard_map/all_to_all | solution.py:262
  67.1 0.0 copy-done.5
  67.1 0.2 collective-permute-start.4
  67.3 1.3 %select.1 = (bf16[96,512]{1,0:T(8,128)(2,1)S(1)}, s32[512,32]{1,0:T(8,128)S(1)}) custom-call(s32[6,32]{1,0:T(8,128)} %bitcast.32, f32[6,32]{1,0:T(8,128)} %bitcast.34), custom_call_target="tpu_custom_call" | custom-call | flops 1048576 | bytes 163840 | tf_op jit(solution)/shard_map/select/pallas_call | solution.py:221
  68.6 1.4 %collective-permute-done.4.act2_ref = bf16[3,704,256]{2,1,0:T(8,128)(2,1)} collective-permute-done((bf16[3,704,256]{2,1,0:T(8,128)(2,1)S(1)}, bf16[3,704,256]{2,1,0:T(8,128)(2,1)}, u32[]{:S(2)}, u32[]{:S(2)}) %collective-permute-start.4) | collective-permute-done | bytes 1081376 | tf_op jit(solution)/shard_map/ppermute | solution.py:266
  70.0 0.0 collective-permute-done.3.rows2_ref
  70.0 0.0 copy-start.3
  70.0 1.6 %copy-done.3 = bf16[2,256,2048]{2,1,0:T(8,128)(2,1)S(1)} copy-done((bf16[2,256,2048]{2,1,0:T(8,128)(2,1)S(1)}, bf16[2,256,2048]{2,1,0:T(8,128)(2,1)}, u32[]{:S(2)}) %copy-start.3) | copy-done | bytes 2097176
  71.6 0.0 copy-start.4
  71.6 1.2 %copy-done.4 = bf16[3,704,256]{2,1,0:T(8,128)(2,1)S(1)} copy-done((bf16[3,704,256]{2,1,0:T(8,128)(2,1)S(1)}, bf16[3,704,256]{2,1,0:T(8,128)(2,1)}, u32[]{:S(2)}) %copy-start.4) | copy-done | bytes 1081368
  72.8 0.0 copy-start
  72.8 9.9 %weight_grads.1 = (bf16[704,2048]{1,0:T(8,128)(2,1)}, bf16[704,2048]{1,0:T(8,128)(2,1)}, bf16[704,2048]{1,0:T(8,128)(2,1)}) custom-call(bf16[2,256,2048]{2,1,0:T(8,128)(2,1)S(1)} %copy-done.3, bf16[3,704,256]{2,1,0:T(8,128)(2,1)S(1)} %copy-done.4, bf16[2,256,2048]{2,1,0:T(8,128)(2,1)} %collective-permute-done.3.rows2_ref, ...), custom_call_target="tpu_custom_call" | custom-call | flops 4429185024 | bytes 8650752 | tf_op jit(solution)/shard_map/weight_grads/pallas_call | solution.py:188
  82.7 14.8 %all-to-all-done.1 = bf16[64,8,2048]{2,1,0:T(8,128)(2,1)S(1)} async-done(((bf16[64,8,2048]{2,1,0:T(8,128)(2,1)}), bf16[64,8,2048]{2,1,0:T(8,128)(2,1)S(1)}, u32[]{:S(2)}, u32[]{:S(2)}) %all-to-all-start.1) | async-done | bytes 2097184 | tf_op jit(solution)/shard_map/all_to_all | solution.py:262
  97.4 0.0 copy-done
  97.4 1.7 %combine.1 = (bf16[32,2048]{1,0:T(8,128)(2,1)}, bf16[32,2048]{1,0:T(8,128)(2,1)}, f32[6,32]{1,0:T(8,128)}) custom-call(bf16[96,512]{1,0:T(8,128)(2,1)S(1)} %get-tuple-element.39.pick_ref, s32[512,32]{1,0:T(8,128)S(1)} %get-tuple-element.40.choice_ref, bf16[32,2048]{1,0:T(8,128)(2,1)S(1)} %copy-done, bf16[512,2048]{1,0:T(8,128)(2,1)S(1)} %bitcast.21), custom_call_target="tpu_custom_call" | custom-call | tf_op jit(solution)/shard_map/combine/pallas_call | solution.py:244
Async XLA Ops:
  0.6 47.7 %collective-permute-start = (bf16[704,2048]{1,0:T(8,128)(2,1)}, bf16[704,2048]{1,0:T(8,128)(2,1)S(1)}, u32[]{:S(2)}, u32[]{:S(2)}) collective-permute-start(bf16[704,2048]{1,0:T(8,128)(2,1)} %bitcast.23), channel_id=1, source_target_pairs={{0,1},{1,0},{2,3},{3,2},{4,5},{5,4},{6,7},{7,6},{8,9},{9,8},{10,11... | collective-permute-start | bytes 8650760 | tf_op jit(solution)/shard_map/ppermute | solution.py:266
  2.1 46.2 %collective-permute-start.1 = (bf16[704,2048]{1,0:T(8,128)(2,1)}, bf16[704,2048]{1,0:T(8,128)(2,1)S(1)}, u32[]{:S(2)}, u32[]{:S(2)}) collective-permute-start(bf16[704,2048]{1,0:T(8,128)(2,1)} %bitcast.25), channel_id=1, source_target_pairs={{0,1},{1,0},{2,3},{3,2},{4,5},{5,4},{6,7},{7,6},{8,9},{9,8},{10,11... | collective-permute-start | bytes 8650760 | tf_op jit(solution)/shard_map/ppermute | solution.py:266
  2.2 46.1 %collective-permute-start.2 = (bf16[704,2048]{1,0:T(8,128)(2,1)}, bf16[704,2048]{1,0:T(8,128)(2,1)S(1)}, u32[]{:S(2)}, u32[]{:S(2)}) collective-permute-start(bf16[704,2048]{1,0:T(8,128)(2,1)} %bitcast.27), channel_id=1, source_target_pairs={{0,1},{1,0},{2,3},{3,2},{4,5},{5,4},{6,7},{7,6},{8,9},{9,8},{10,11... | collective-permute-start | bytes 8650760 | tf_op jit(solution)/shard_map/ppermute | solution.py:266
  2.6 45.7 %copy-start.2 = (bf16[1,2048,704]{1,2,0:T(8,128)(2,1)S(1)}, bf16[1,2048,704]{1,2,0:T(8,128)(2,1)}, u32[]{:S(2)}) copy-start(bf16[1,2048,704]{1,2,0:T(8,128)(2,1)} %param.12) | copy-start | bytes 8650756
  6.6 41.7 %copy-start.1 = (bf16[1,2048,704]{1,2,0:T(8,128)(2,1)S(1)}, bf16[1,2048,704]{1,2,0:T(8,128)(2,1)}, u32[]{:S(2)}) copy-start(bf16[1,2048,704]{1,2,0:T(8,128)(2,1)} %param.11) | copy-start | bytes 8650756
  60.7 6.3 %copy-start.5 = (bf16[3,704,256]{2,1,0:T(8,128)(2,1)S(1)}, bf16[3,704,256]{2,1,0:T(8,128)(2,1)}, u32[]{:S(2)}) copy-start(bf16[3,704,256]{2,1,0:T(8,128)(2,1)} %get-tuple-element.35) | copy-start | bytes 3244036
  60.7 9.3 %collective-permute-start.3 = (bf16[2,256,2048]{2,1,0:T(8,128)(2,1)}, bf16[2,256,2048]{2,1,0:T(8,128)(2,1)}, u32[]{:S(2)}, u32[]{:S(2)}) collective-permute-start(bf16[2,256,2048]{2,1,0:T(8,128)(2,1)} %get-tuple-element.33.rows_ref), channel_id=1, source_target_pairs={{0,1},{1,0},{2,3},{3,2},{4,5},{5,4},{6,7},{7,6},{8,9},{9,8},{10,11... | collective-permute-start | bytes 6291464 | tf_op jit(solution)/shard_map/ppermute | solution.py:266
  62.4 35.1 %all-to-all-start.1 = ((bf16[64,8,2048]{2,1,0:T(8,128)(2,1)}), bf16[64,8,2048]{2,1,0:T(8,128)(2,1)S(1)}, u32[]{:S(2)}, u32[]{:S(2)}) async-start(bf16[64,8,2048]{2,1,0:T(8,128)(2,1)} %bitcast.29), calls=%async_computation.1 | async-start | bytes 4194304 | tf_op jit(solution)/shard_map/all_to_all | solution.py:262
  67.1 2.9 %collective-permute-start.4 = (bf16[3,704,256]{2,1,0:T(8,128)(2,1)S(1)}, bf16[3,704,256]{2,1,0:T(8,128)(2,1)}, u32[]{:S(2)}, u32[]{:S(2)}) collective-permute-start(bf16[3,704,256]{2,1,0:T(8,128)(2,1)S(1)} %copy-done.5), channel_id=1, source_target_pairs={{0,1},{1,0},{2,3},{3,2},{4,5},{5,4},{6,7},{7,6},{8,9},{9,8},{10,11... | collective-permute-start | bytes 3244040 | tf_op jit(solution)/shard_map/ppermute | solution.py:266
  70.0 1.6 %copy-start.3 = (bf16[2,256,2048]{2,1,0:T(8,128)(2,1)S(1)}, bf16[2,256,2048]{2,1,0:T(8,128)(2,1)}, u32[]{:S(2)}) copy-start(bf16[2,256,2048]{2,1,0:T(8,128)(2,1)} %get-tuple-element.33.rows_ref) | copy-start | bytes 6291460
  71.6 1.2 %copy-start.4 = (bf16[3,704,256]{2,1,0:T(8,128)(2,1)S(1)}, bf16[3,704,256]{2,1,0:T(8,128)(2,1)}, u32[]{:S(2)}) copy-start(bf16[3,704,256]{2,1,0:T(8,128)(2,1)} %get-tuple-element.34.act_ref) | copy-start | bytes 3244036
  72.8 24.6 %copy-start = (bf16[32,2048]{1,0:T(8,128)(2,1)S(1)}, bf16[32,2048]{1,0:T(8,128)(2,1)}, u32[]{:S(2)}) copy-start(bf16[32,2048]{1,0:T(8,128)(2,1)} %cot_ref.1) | copy-start | bytes 393220

commit v3 on v2

--- a/solution.py
+++ b/solution.py
@@ -40,10 +40,10 @@
     return expert, is_dy, fills, gate
 
 
-def pack_kernel(ids_hbm, gates_hbm, tok_hbm, cot_hbm, w_hbm, out_hbm, w_ref, *refs):
-    ids_ref, gates_ref, both_ref, packed, in_sem, out_sem = refs
-    steps = out_sem.shape[0]
-    rows, toks = packed.shape[0] // steps, tok_hbm.shape[0]
+def pack_kernel(ids_hbm, gates_hbm, tok_hbm, cot_hbm, w_hbm, out_ref, w_ref, *refs):
+    ids_ref, gates_ref, both_ref, in_sem = refs
+    steps = 4
+    rows, toks = out_ref.shape[0] // steps, tok_hbm.shape[0]
     pairs = (
         (ids_hbm, ids_ref),
         (gates_hbm, gates_ref),
@@ -57,19 +57,13 @@
     for load in loads[:4]:
         load.wait()
     both = both_ref[...]
-    copies = []
     for i in range(steps):
         _, is_dy, fills, gate = routing(ids_ref[...], gates_ref[...], i * rows, rows)
         pick_x = jnp.where(fills & ~is_dy, 1.0, 0.0)
         pick_dy = jnp.where(fills & is_dy, 1.0, 0.0)
         scale = jnp.sum(pick_x + pick_dy * gate, axis=1, keepdims=True)
         pick = jnp.concatenate([pick_x, pick_dy], axis=1).astype(BF16)
-        s = slice(i * rows, (i + 1) * rows)
-        packed[s, :] = (mm(pick, both) * scale).astype(BF16)
-        copies.append(pltpu.make_async_copy(packed.at[s], out_hbm.at[s], out_sem.at[i]))
-        copies[-1].start()
-    for copy in copies:
-        copy.wait()
+        out_ref[i * rows : (i + 1) * rows, :] = (mm(pick, both) * scale).astype(BF16)
     loads[4].wait()
 
 
@@ -78,15 +72,13 @@
     return pl.pallas_call(
         pack_kernel,
         in_specs=[HBM] * 5,
-        out_specs=[HBM, VMEM],
-        out_shape=[pltpu.HBM((rows, width), BF16), pltpu.VMEM(weight.shape, BF16)],
+        out_specs=[VMEM, VMEM],
+        out_shape=[pltpu.VMEM((rows, width), BF16), pltpu.VMEM(weight.shape, BF16)],
         scratch_shapes=[
             pltpu.VMEM(ids.shape, I32),
             pltpu.VMEM(gates.shape, F32),
             pltpu.VMEM((2 * tokens.shape[0], width), BF16),
-            pltpu.VMEM((rows, width), BF16),
             pltpu.SemaphoreType.DMA((5,)),
-            pltpu.SemaphoreType.DMA((4,)),
         ],
         cost_estimate=pl.CostEstimate(
             flops=4 * rows * width * ids.shape[1], bytes_accessed=2 * rows * width, transcendentals=0
@@ -96,13 +88,23 @@
     )(*(pltpu.with_memory_space_constraint(a, pltpu.HBM) for a in (ids, gates, tokens, cot, weight)))
 
 
-def deal(size):
-    i = lax.broadcasted_iota(I32, (size, size), 0)
-    q = lax.broadcasted_iota(I32, (size, size), 1)
-    half = size // 2
-    r = i % half
-    source = (r // CAP) * 2 * CAP + r % CAP + jnp.where(i >= half, CAP, 0)
-    return jnp.where(source == q, 1.0, 0.0).astype(BF16)
+def split(both):
+    rows, cols = both.shape
+    pairs = both.reshape(rows // (4 * CAP), 2, 2 * CAP, cols)
+    even, odd = pairs[:, 0], pairs[:, 1]
+    first = lax.broadcasted_iota(I32, even.shape, 1) < CAP
+    x = jnp.where(first, even, pltpu.roll(odd, CAP, 1))
+    dy = jnp.where(first, pltpu.roll(even, CAP, 1), odd)
+    return x.reshape(rows // 2, cols), dy.reshape(rows // 2, cols)
+
+
+def merge(p, q):
+    rows, cols = p.shape
+    p, q = (a.reshape(rows // (2 * CAP), 2 * CAP, cols) for a in (p, q))
+    first = lax.broadcasted_iota(I32, p.shape, 1) < CAP
+    even = jnp.where(first, p, pltpu.roll(q, CAP, 1))
+    odd = jnp.where(first, pltpu.roll(p, CAP, 1), q)
+    return jnp.stack([even, odd], axis=1).reshape(2 * rows, cols)
 
 
 def expert_kernel(z_ref, wg, wu, wd, wg2, wu2, wd2, rows_hbm, act_hbm, act2_hbm, sent_hbm, *refs):
@@ -110,11 +112,11 @@
     part, tile, cols = 256, 352, 512
     rows, width = z_ref.shape
     hid = wg.shape[0]
-    perm = deal(part)
     for m in range(rows // part):
-        dealt = mm(perm, z_ref[m * part : (m + 1) * part, :]).astype(BF16)
-        rows_ref[0, m * part // 2 : (m + 1) * part // 2, :] = dealt[: part // 2]
-        rows_ref[1, m * part // 2 : (m + 1) * part // 2, :] = dealt[part // 2 :]
+        r = slice(m * part // 2, (m + 1) * part // 2)
+        x, dy = split(z_ref[m * part : (m + 1) * part, :].astype(F32))
+        rows_ref[0, r, :] = x.astype(BF16)
+        rows_ref[1, r, :] = dy.astype(BF16)
     copies = []
 
     def send(source, target):
@@ -140,11 +142,7 @@
         p = mm(act[0, 0], wd[:, c], TN) + mm(act[1, 0], wd2[:, c], TN)
         q = mm(act[0, 1], wg[:, c], TN) + mm(act[1, 1], wg2[:, c], TN)
         q = q + mm(act[0, 2], wu[:, c], TN) + mm(act[1, 2], wu2[:, c], TN)
-        p, q = p.astype(BF16), q.astype(BF16)
-        for m in range(rows // part):
-            r = slice(m * part // 2, (m + 1) * part // 2)
-            both = jnp.concatenate([p[r], q[r]], axis=0)
-            sent[m * part : (m + 1) * part, c] = mm(perm, both, TN).astype(BF16)
+        sent[:, c] = merge(p, q).astype(BF16)
         send(sent.at[:, c], sent_hbm.at[:, c])
     for copy in copies:
         copy.wait()
@@ -199,7 +197,7 @@
     )(rows, act, rows2, act2)
 
 
-def select_kernel(ids_ref, gates_ref, pick_ref, choice_ref):
+def select_kernel(ids_ref, gates_ref, after_hbm, pick_ref, choice_ref):
     ids = ids_ref[...]
     top, toks = ids.shape
     rows = choice_ref.shape[0]
@@ -216,16 +214,16 @@
     choice_ref[...] = jnp.where(fills & ~is_dy, choice, -1)
 
 
-def select(ids, gates, experts):
+def select(ids, gates, experts, after):
     rows, toks = experts * 2 * CAP, ids.shape[1]
     return pl.pallas_call(
         select_kernel,
-        in_specs=[VMEM] * 2,
+        in_specs=[VMEM] * 2 + [HBM],
         out_specs=[VMEM] * 2,
         out_shape=[pltpu.VMEM((3 * toks, rows), BF16), pltpu.VMEM((rows, toks), I32)],
         cost_estimate=pl.CostEstimate(flops=rows * toks * 64, bytes_accessed=rows * toks * 10, transcendentals=0),
         name="select",
-    )(ids, gates)
+    )(ids, gates, pltpu.with_memory_space_constraint(after, pltpu.HBM))
 
 
 def combine_kernel(pick_ref, choice_ref, cot_ref, back_ref, mixed_ref, dtok_ref, dgates_ref):
@@ -274,10 +272,9 @@
     packed, down = pack(ids, gates, tokens, cotangent, mine[2], experts)
     z = route(packed)
     rows, act, act_theirs, sent = expert(z, (*mine[:2], down), theirs)
+    back = route(sent)
+    pick, choice = select(ids, gates, experts, sent)
     rows2, act2 = swap(rows), swap(act_theirs)
-    back = route(sent)
-    ids, gates, _ = lax.optimization_barrier((ids, gates, sent[:8, :128]))
-    pick, choice = select(ids, gates, experts)
     grads = weight_grads(rows, act, rows2, act2)
     pick, choice, grad_gate, grad_up, grad_down = lax.optimization_barrier((pick, choice, *grads))
     mixed, d_tokens, d_gates = combine(pick, choice, cotangent, back, ids.shape[0])

time: 99.8 us -> 96.9 us (0.971)
  Pallas kernels: 29.1 us -> 26.6 us
    pallas_call x1, Pallas kernels: 12.3 us -> 10.9 us  [expert(): pl.pallas_call(expert_kernel, in_specs=[VMEM] * 7, out_specs=[HBM] * 4, o...]
    pallas_call x2, Pallas kernels: 5.26 us -> 4.1 us  [the longest x1 2.83 us: pack(): pl.pallas_call(pack_kernel, in_specs=[HBM] * 5, out_specs=[VMEM, VMEM], o...]
  transfers between devices with their start and end apart: 6 -> 6, of which waited for: 2 -> 2; matrix products, arithmetic and copies ran while one was open for 0% -> 0% of each run, Pallas kernels for 15% -> 14%
where the time goes in v3:
time: 96.9 us; the launch traced here: 96.4 us
  blocking collectives  41.5 us (43%)
  Pallas kernels  26.6 us (27%)
  waiting for transfers between devices  16.2 us (17%)
  starting transfers between devices  8.57 us (9%)
  local copies, waits for them, and re-layouts  2.85 us (3%)
    all_to_all x1, blocking collectives, route(): lax.all_to_all(blocks, ('expert', 'chip'), 0, 0, tiled=True)  41.5 us
    all_to_all x1, waiting for transfers between devices, route(): lax.all_to_all(blocks, ('expert', 'chip'), 0, 0, tiled=True)  14.8 us
    pallas_call x1, Pallas kernels, expert(): pl.pallas_call(expert_kernel, in_specs=[VMEM] * 7, out_specs=[HBM] * 4, o...  10.9 us
    pallas_call x1, Pallas kernels, weight_grads(): pl.pallas_call(weight_grads_kernel, grid=(width // cols,), in_specs=[tall...  9.88 us
    all_to_all x1, starting transfers between devices, route(): lax.all_to_all(blocks, ('expert', 'chip'), 0, 0, tiled=True)  4.69 us
    ppermute x5, starting transfers between devices, swap(): return lax.ppermute(rows, 'core', [(0, 1), (1, 0)])  3.88 us
    unnamed x12, local copies, waits for them, and re-layouts  2.85 us
    pallas_call x1, Pallas kernels, pack(): pl.pallas_call(pack_kernel, in_specs=[HBM] * 5, out_specs=[VMEM, VMEM], o...  2.83 us
  transfers between devices with their start and end apart: 6, of which 2 were waited for; matrix products, arithmetic and copies ran while one was open for 0% of the time, Pallas kernels for 14%

profile of v3, /device:TPU:1, one launch (start us, length us, event | category | flops | bytes accessed | tf_op | source)
XLA Modules:
  0.0 96.4 jit_solution(10290173168586908159)
XLA Ops:
  0.6 1.5 %collective-permute-start = (bf16[704,2048]{1,0:T(8,128)(2,1)}, bf16[704,2048]{1,0:T(8,128)(2,1)S(1)}, u32[]{:S(2)}, u32[]{:S(2)}) collective-permute-start(bf16[704,2048]{1,0:T(8,128)(2,1)} %bitcast.24), channel_id=1, source_target_pairs={{0,1},{1,0},{2,3},{3,2},{4,5},{5,4},{6,7},{7,6},{8,9},{9,8},{10,11... | collective-permute-start | bytes 8650760 | tf_op jit(solution)/shard_map/ppermute | solution.py:264
  2.1 0.1 collective-permute-start.1
  2.2 0.4 collective-permute-start.2
  2.6 0.0 copy-start.2
  2.6 2.8 %pack.1 = (bf16[512,2048]{1,0:T(8,128)(2,1)S(1)}, bf16[704,2048]{1,0:T(8,128)(2,1)S(1)}) custom-call(s32[6,32]{1,0:T(8,128)} %bitcast.31, f32[6,32]{1,0:T(8,128)} %bitcast.33, bf16[32,2048]{1,0:T(8,128)(2,1)} %tok_hbm.1, bf16[32,2048]{1,0:T(8,128)(2,1)} %cot_ref.1, bf16[704,2048]{1,0:T(8,128)(2,1)} %bitcast.30), custom_call_target="tpu_custom_call" | custom-call | flops 134217728 | bytes 2097152 | tf_op jit(solution)/shard_map/pack/pallas_call | solution.py:72
  5.5 0.0 copy-start.1
  5.5 41.5 %all_to_all.10 = bf16[64,8,2048]{2,1,0:T(8,128)(2,1)S(1)} all-to-all(bf16[64,8,2048]{2,1,0:T(8,128)(2,1)S(1)} %bitcast.23), channel_id=1, replica_groups=mesh['expert'=4,'chip'=16,'core'=2] {'expert','chip'}, dimensions={0} | all-to-all | bytes 4194304 | tf_op jit(solution)/shard_map/all_to_all | solution.py:260
  47.0 0.0 collective-permute-done.wg2
  47.0 0.0 collective-permute-done.1.wu2
  47.0 0.0 collective-permute-done.2.wd2
  47.0 0.0 copy-done.2
  47.0 0.0 copy-done.1
  47.0 10.9 %expert.1 = (bf16[2,256,2048]{2,1,0:T(8,128)(2,1)}, bf16[3,704,256]{2,1,0:T(8,128)(2,1)}, bf16[3,704,256]{2,1,0:T(8,128)(2,1)}, bf16[512,2048]{1,0:T(8,128)(2,1)}) custom-call(bf16[512,2048]{1,0:T(8,128)(2,1)S(1)} %bitcast.22, bf16[704,2048]{1,0:T(8,128)(2,1)S(1)} %bitcast.25, bf16[704,2048]{1,0:T(8,128)(2,1)S(1)} %bitcast.27, ...), custom_call_target="tpu_custom_call" | custom-call | flops 8858370048 | bytes 17301504 | tf_op jit(solution)/shard_map/expert/pallas_call | solution.py:155
  57.9 0.0 copy-start.5
  58.0 1.6 %collective-permute-start.3 = (bf16[2,256,2048]{2,1,0:T(8,128)(2,1)}, bf16[2,256,2048]{2,1,0:T(8,128)(2,1)}, u32[]{:S(2)}, u32[]{:S(2)}) collective-permute-start(bf16[2,256,2048]{2,1,0:T(8,128)(2,1)} %get-tuple-element.30.rows_ref), channel_id=1, source_target_pairs={{0,1},{1,0},{2,3},{3,2},{4,5},{5,4},{6,7},{7,6},{8,9},{9,8},{10,11... | collective-permute-start | bytes 6291464 | tf_op jit(solution)/shard_map/ppermute | solution.py:264
  59.6 4.7 %all-to-all-start.1 = ((bf16[64,8,2048]{2,1,0:T(8,128)(2,1)}), bf16[64,8,2048]{2,1,0:T(8,128)(2,1)S(1)}, u32[]{:S(2)}, u32[]{:S(2)}) async-start(bf16[64,8,2048]{2,1,0:T(8,128)(2,1)} %bitcast.28), calls=%async_computation.1 | async-start | bytes 4194304 | tf_op jit(solution)/shard_map/all_to_all | solution.py:260
  64.3 0.0 copy-done.5
  64.3 0.2 collective-permute-start.4
  64.5 1.3 %select.1 = (bf16[96,512]{1,0:T(8,128)(2,1)S(1)}, s32[512,32]{1,0:T(8,128)S(1)}) custom-call(s32[6,32]{1,0:T(8,128)} %bitcast.32, f32[6,32]{1,0:T(8,128)} %bitcast.34, bf16[512,2048]{1,0:T(8,128)(2,1)} %get-tuple-element.27.after_hbm), custom_call_target="tpu_custom_call" | custom-call | flops 1048576 | bytes 163840 | tf_op jit(solution)/shard_map/select/pallas_call | solution.py:219
  65.8 1.4 %collective-permute-done.4.act2_ref = bf16[3,704,256]{2,1,0:T(8,128)(2,1)} collective-permute-done((bf16[3,704,256]{2,1,0:T(8,128)(2,1)S(1)}, bf16[3,704,256]{2,1,0:T(8,128)(2,1)}, u32[]{:S(2)}, u32[]{:S(2)}) %collective-permute-start.4) | collective-permute-done | bytes 1081376 | tf_op jit(solution)/shard_map/ppermute | solution.py:264
  67.2 0.0 collective-permute-done.3.rows2_ref
  67.2 0.0 copy-start.3
  67.2 1.6 %copy-done.3 = bf16[2,256,2048]{2,1,0:T(8,128)(2,1)S(1)} copy-done((bf16[2,256,2048]{2,1,0:T(8,128)(2,1)S(1)}, bf16[2,256,2048]{2,1,0:T(8,128)(2,1)}, u32[]{:S(2)}) %copy-start.3) | copy-done | bytes 2097176
  68.8 0.0 copy-start.4
  68.8 1.2 %copy-done.4 = bf16[3,704,256]{2,1,0:T(8,128)(2,1)S(1)} copy-done((bf16[3,704,256]{2,1,0:T(8,128)(2,1)S(1)}, bf16[3,704,256]{2,1,0:T(8,128)(2,1)}, u32[]{:S(2)}) %copy-start.4) | copy-done | bytes 1081368
  70.0 0.0 copy-start
  70.0 9.9 %weight_grads.1 = (bf16[704,2048]{1,0:T(8,128)(2,1)}, bf16[704,2048]{1,0:T(8,128)(2,1)}, bf16[704,2048]{1,0:T(8,128)(2,1)}) custom-call(bf16[2,256,2048]{2,1,0:T(8,128)(2,1)S(1)} %copy-done.3, bf16[3,704,256]{2,1,0:T(8,128)(2,1)S(1)} %copy-done.4, bf16[2,256,2048]{2,1,0:T(8,128)(2,1)} %collective-permute-done.3.rows2_ref, ...), custom_call_target="tpu_custom_call" | custom-call | flops 4429185024 | bytes 8650752 | tf_op jit(solution)/shard_map/weight_grads/pallas_call | solution.py:186
  79.9 14.8 %all-to-all-done.1 = bf16[64,8,2048]{2,1,0:T(8,128)(2,1)S(1)} async-done(((bf16[64,8,2048]{2,1,0:T(8,128)(2,1)}), bf16[64,8,2048]{2,1,0:T(8,128)(2,1)S(1)}, u32[]{:S(2)}, u32[]{:S(2)}) %all-to-all-start.1) | async-done | bytes 2097184 | tf_op jit(solution)/shard_map/all_to_all | solution.py:260
  94.7 0.0 copy-done
  94.7 1.7 %combine.1 = (bf16[32,2048]{1,0:T(8,128)(2,1)}, bf16[32,2048]{1,0:T(8,128)(2,1)}, f32[6,32]{1,0:T(8,128)}) custom-call(bf16[96,512]{1,0:T(8,128)(2,1)S(1)} %get-tuple-element.36.pick_ref, s32[512,32]{1,0:T(8,128)S(1)} %get-tuple-element.37.choice_ref, bf16[32,2048]{1,0:T(8,128)(2,1)S(1)} %copy-done, bf16[512,2048]{1,0:T(8,128)(2,1)S(1)} %bitcast.21), custom_call_target="tpu_custom_call" | custom-call | tf_op jit(solution)/shard_map/combine/pallas_call | solution.py:242
Async XLA Ops:
  0.6 46.4 %collective-permute-start = (bf16[704,2048]{1,0:T(8,128)(2,1)}, bf16[704,2048]{1,0:T(8,128)(2,1)S(1)}, u32[]{:S(2)}, u32[]{:S(2)}) collective-permute-start(bf16[704,2048]{1,0:T(8,128)(2,1)} %bitcast.24), channel_id=1, source_target_pairs={{0,1},{1,0},{2,3},{3,2},{4,5},{5,4},{6,7},{7,6},{8,9},{9,8},{10,11... | collective-permute-start | bytes 8650760 | tf_op jit(solution)/shard_map/ppermute | solution.py:264
  2.1 44.9 %collective-permute-start.1 = (bf16[704,2048]{1,0:T(8,128)(2,1)}, bf16[704,2048]{1,0:T(8,128)(2,1)S(1)}, u32[]{:S(2)}, u32[]{:S(2)}) collective-permute-start(bf16[704,2048]{1,0:T(8,128)(2,1)} %bitcast.26), channel_id=1, source_target_pairs={{0,1},{1,0},{2,3},{3,2},{4,5},{5,4},{6,7},{7,6},{8,9},{9,8},{10,11... | collective-permute-start | bytes 8650760 | tf_op jit(solution)/shard_map/ppermute | solution.py:264
  2.2 44.8 %collective-permute-start.2 = (bf16[704,2048]{1,0:T(8,128)(2,1)}, bf16[704,2048]{1,0:T(8,128)(2,1)S(1)}, u32[]{:S(2)}, u32[]{:S(2)}) collective-permute-start(bf16[704,2048]{1,0:T(8,128)(2,1)} %bitcast.29), channel_id=1, source_target_pairs={{0,1},{1,0},{2,3},{3,2},{4,5},{5,4},{6,7},{7,6},{8,9},{9,8},{10,11... | collective-permute-start | bytes 8650760 | tf_op jit(solution)/shard_map/ppermute | solution.py:264
  2.6 44.4 %copy-start.2 = (bf16[1,2048,704]{1,2,0:T(8,128)(2,1)S(1)}, bf16[1,2048,704]{1,2,0:T(8,128)(2,1)}, u32[]{:S(2)}) copy-start(bf16[1,2048,704]{1,2,0:T(8,128)(2,1)} %param.12) | copy-start | bytes 8650756
  5.5 41.5 %copy-start.1 = (bf16[1,2048,704]{1,2,0:T(8,128)(2,1)S(1)}, bf16[1,2048,704]{1,2,0:T(8,128)(2,1)}, u32[]{:S(2)}) copy-start(bf16[1,2048,704]{1,2,0:T(8,128)(2,1)} %param.11) | copy-start | bytes 8650756
  57.9 6.3 %copy-start.5 = (bf16[3,704,256]{2,1,0:T(8,128)(2,1)S(1)}, bf16[3,704,256]{2,1,0:T(8,128)(2,1)}, u32[]{:S(2)}) copy-start(bf16[3,704,256]{2,1,0:T(8,128)(2,1)} %get-tuple-element.32) | copy-start | bytes 3244036
  58.0 9.3 %collective-permute-start.3 = (bf16[2,256,2048]{2,1,0:T(8,128)(2,1)}, bf16[2,256,2048]{2,1,0:T(8,128)(2,1)}, u32[]{:S(2)}, u32[]{:S(2)}) collective-permute-start(bf16[2,256,2048]{2,1,0:T(8,128)(2,1)} %get-tuple-element.30.rows_ref), channel_id=1, source_target_pairs={{0,1},{1,0},{2,3},{3,2},{4,5},{5,4},{6,7},{7,6},{8,9},{9,8},{10,11... | collective-permute-start | bytes 6291464 | tf_op jit(solution)/shard_map/ppermute | solution.py:264
  59.6 35.1 %all-to-all-start.1 = ((bf16[64,8,2048]{2,1,0:T(8,128)(2,1)}), bf16[64,8,2048]{2,1,0:T(8,128)(2,1)S(1)}, u32[]{:S(2)}, u32[]{:S(2)}) async-start(bf16[64,8,2048]{2,1,0:T(8,128)(2,1)} %bitcast.28), calls=%async_computation.1 | async-start | bytes 4194304 | tf_op jit(solution)/shard_map/all_to_all | solution.py:260
  64.3 2.9 %collective-permute-start.4 = (bf16[3,704,256]{2,1,0:T(8,128)(2,1)S(1)}, bf16[3,704,256]{2,1,0:T(8,128)(2,1)}, u32[]{:S(2)}, u32[]{:S(2)}) collective-permute-start(bf16[3,704,256]{2,1,0:T(8,128)(2,1)S(1)} %copy-done.5), channel_id=1, source_target_pairs={{0,1},{1,0},{2,3},{3,2},{4,5},{5,4},{6,7},{7,6},{8,9},{9,8},{10,11... | collective-permute-start | bytes 3244040 | tf_op jit(solution)/shard_map/ppermute | solution.py:264
  67.2 1.6 %copy-start.3 = (bf16[2,256,2048]{2,1,0:T(8,128)(2,1)S(1)}, bf16[2,256,2048]{2,1,0:T(8,128)(2,1)}, u32[]{:S(2)}) copy-start(bf16[2,256,2048]{2,1,0:T(8,128)(2,1)} %get-tuple-element.30.rows_ref) | copy-start | bytes 6291460
  68.8 1.2 %copy-start.4 = (bf16[3,704,256]{2,1,0:T(8,128)(2,1)S(1)}, bf16[3,704,256]{2,1,0:T(8,128)(2,1)}, u32[]{:S(2)}) copy-start(bf16[3,704,256]{2,1,0:T(8,128)(2,1)} %get-tuple-element.31.act_ref) | copy-start | bytes 3244036
  70.0 24.6 %copy-start = (bf16[32,2048]{1,0:T(8,128)(2,1)S(1)}, bf16[32,2048]{1,0:T(8,128)(2,1)}, u32[]{:S(2)}) copy-start(bf16[32,2048]{1,0:T(8,128)(2,1)} %cot_ref.1) | copy-start | bytes 393220

commit v4 on v3

--- a/solution.py
+++ b/solution.py
@@ -42,8 +42,7 @@
 
 def pack_kernel(ids_hbm, gates_hbm, tok_hbm, cot_hbm, w_hbm, out_ref, w_ref, *refs):
     ids_ref, gates_ref, both_ref, in_sem = refs
-    steps = 4
-    rows, toks = out_ref.shape[0] // steps, tok_hbm.shape[0]
+    rows, toks = out_ref.shape[0], tok_hbm.shape[0]
     pairs = (
         (ids_hbm, ids_ref),
         (gates_hbm, gates_ref),
@@ -56,14 +55,12 @@
         load.start()
     for load in loads[:4]:
         load.wait()
-    both = both_ref[...]
-    for i in range(steps):
-        _, is_dy, fills, gate = routing(ids_ref[...], gates_ref[...], i * rows, rows)
-        pick_x = jnp.where(fills & ~is_dy, 1.0, 0.0)
-        pick_dy = jnp.where(fills & is_dy, 1.0, 0.0)
-        scale = jnp.sum(pick_x + pick_dy * gate, axis=1, keepdims=True)
-        pick = jnp.concatenate([pick_x, pick_dy], axis=1).astype(BF16)
-        out_ref[i * rows : (i + 1) * rows, :] = (mm(pick, both) * scale).astype(BF16)
+    _, is_dy, fills, gate = routing(ids_ref[...], gates_ref[...], 0, rows)
+    pick_x = jnp.where(fills & ~is_dy, 1.0, 0.0)
+    pick_dy = jnp.where(fills & is_dy, 1.0, 0.0)
+    scale = jnp.sum(pick_x + pick_dy * gate, axis=1, keepdims=True)
+    pick = jnp.concatenate([pick_x, pick_dy], axis=1).astype(BF16)
+    out_ref[...] = (mm(pick, both_ref[...]) * scale).astype(BF16)
     loads[4].wait()
 
 
@@ -226,27 +223,36 @@
     )(ids, gates, pltpu.with_memory_space_constraint(after, pltpu.HBM))
 
 
-def combine_kernel(pick_ref, choice_ref, cot_ref, back_ref, mixed_ref, dtok_ref, dgates_ref):
+def combine_kernel(pick_ref, choice_ref, cot_ref, back_ref, mixed_hbm, dtok_hbm, dgates_hbm, out, dgates, sem):
     toks = cot_ref.shape[0]
     back = back_ref[...]
     sums = mm(pick_ref[...], back)
-    mixed_ref[...] = (sums[:toks] + sums[toks : 2 * toks]).astype(BF16)
-    dtok_ref[...] = sums[2 * toks :].astype(BF16)
+    out[0] = (sums[:toks] + sums[toks : 2 * toks]).astype(BF16)
+    out[1] = sums[2 * toks :].astype(BF16)
+    pairs = ((out.at[0], mixed_hbm), (out.at[1], dtok_hbm), (dgates, dgates_hbm))
+    copies = [pltpu.make_async_copy(source, target, sem.at[i]) for i, (source, target) in enumerate(pairs)]
+    for copy in copies[:2]:
+        copy.start()
     inner = mm(back, cot_ref[...], NT)
     choice = choice_ref[...]
-    for k in range(dgates_ref.shape[0]):
-        dgates_ref[k : k + 1, :] = jnp.sum(jnp.where(choice == k, inner, 0.0), axis=0, keepdims=True)
+    for k in range(dgates.shape[0]):
+        dgates[k : k + 1, :] = jnp.sum(jnp.where(choice == k, inner, 0.0), axis=0, keepdims=True)
+    copies[2].start()
+    for copy in copies:
+        copy.wait()
 
 
 def combine(pick, choice, cot, back, top):
+    toks, width = cot.shape
     return pl.pallas_call(
         combine_kernel,
         in_specs=[VMEM] * 4,
-        out_specs=[VMEM] * 3,
-        out_shape=[
-            jax.ShapeDtypeStruct(cot.shape, BF16),
-            jax.ShapeDtypeStruct(cot.shape, BF16),
-            jax.ShapeDtypeStruct((top, cot.shape[0]), F32),
+        out_specs=[HBM] * 3,
+        out_shape=[pltpu.HBM((toks, width), BF16), pltpu.HBM((toks, width), BF16), pltpu.HBM((top, toks), F32)],
+        scratch_shapes=[
+            pltpu.VMEM((2, toks, width), BF16),
+            pltpu.VMEM((top, toks), F32),
+            pltpu.SemaphoreType.DMA((3,)),
         ],
         compiler_params=pltpu.CompilerParams(vmem_limit_bytes=32 << 20),
         name="combine",

time: 96.9 us -> 96.7 us (level)
  no operation moved by 1% of the time
where the time goes in v4:
time: 96.7 us; the launch traced here: 96.1 us
  blocking collectives  41.5 us (43%)
  Pallas kernels  26.2 us (27%)
  waiting for transfers between devices  16.2 us (17%)
  starting transfers between devices  8.58 us (9%)
  local copies, waits for them, and re-layouts  2.85 us (3%)
    all_to_all x1, blocking collectives, route(): lax.all_to_all(blocks, ('expert', 'chip'), 0, 0, tiled=True)  41.5 us
    all_to_all x1, waiting for transfers between devices, route(): lax.all_to_all(blocks, ('expert', 'chip'), 0, 0, tiled=True)  14.8 us
    pallas_call x1, Pallas kernels, expert(): pl.pallas_call(expert_kernel, in_specs=[VMEM] * 7, out_specs=[HBM] * 4, o...  10.9 us
    pallas_call x1, Pallas kernels, weight_grads(): pl.pallas_call(weight_grads_kernel, grid=(width // cols,), in_specs=[tall...  9.87 us
    all_to_all x1, starting transfers between devices, route(): lax.all_to_all(blocks, ('expert', 'chip'), 0, 0, tiled=True)  4.69 us
    ppermute x5, starting transfers between devices, swap(): return lax.ppermute(rows, 'core', [(0, 1), (1, 0)])  3.89 us
    unnamed x12, local copies, waits for them, and re-layouts  2.85 us
    pallas_call x1, Pallas kernels, pack(): pl.pallas_call(pack_kernel, in_specs=[HBM] * 5, out_specs=[VMEM, VMEM], o...  2.4 us
  transfers between devices with their start and end apart: 6, of which 2 were waited for; matrix products, arithmetic and copies ran while one was open for 0% of the time, Pallas kernels for 14%

profile of v4, /device:TPU:1, one launch (start us, length us, event | category | flops | bytes accessed | tf_op | source)
XLA Modules:
  0.0 96.1 jit_solution(16515867122664152327)
XLA Ops:
  0.6 1.5 %collective-permute-start = (bf16[704,2048]{1,0:T(8,128)(2,1)}, bf16[704,2048]{1,0:T(8,128)(2,1)S(1)}, u32[]{:S(2)}, u32[]{:S(2)}) collective-permute-start(bf16[704,2048]{1,0:T(8,128)(2,1)} %bitcast.24), channel_id=1, source_target_pairs={{0,1},{1,0},{2,3},{3,2},{4,5},{5,4},{6,7},{7,6},{8,9},{9,8},{10,11... | collective-permute-start | bytes 8650760 | tf_op jit(solution)/shard_map/ppermute | solution.py:270
  2.1 0.1 collective-permute-start.1
  2.2 0.4 collective-permute-start.2
  2.6 0.0 copy-start.2
  2.6 2.4 %pack.1 = (bf16[512,2048]{1,0:T(8,128)(2,1)S(1)}, bf16[704,2048]{1,0:T(8,128)(2,1)S(1)}) custom-call(s32[6,32]{1,0:T(8,128)} %bitcast.31, f32[6,32]{1,0:T(8,128)} %bitcast.33, bf16[32,2048]{1,0:T(8,128)(2,1)} %tok_hbm.1, bf16[32,2048]{1,0:T(8,128)(2,1)} %cot_ref.1, bf16[704,2048]{1,0:T(8,128)(2,1)} %bitcast.30), custom_call_target="tpu_custom_call" | custom-call | flops 134217728 | bytes 2097152 | tf_op jit(solution)/shard_map/pack/pallas_call | solution.py:69
  5.1 0.0 copy-start.1
  5.1 41.5 %all_to_all.10 = bf16[64,8,2048]{2,1,0:T(8,128)(2,1)S(1)} all-to-all(bf16[64,8,2048]{2,1,0:T(8,128)(2,1)S(1)} %bitcast.23), channel_id=1, replica_groups=mesh['expert'=4,'chip'=16,'core'=2] {'expert','chip'}, dimensions={0} | all-to-all | bytes 4194304 | tf_op jit(solution)/shard_map/all_to_all | solution.py:266
  46.5 0.0 collective-permute-done.wg2
  46.6 0.0 collective-permute-done.1.wu2
  46.6 0.0 collective-permute-done.2.wd2
  46.6 0.0 copy-done.2
  46.6 0.0 copy-done.1
  46.6 10.9 %expert.1 = (bf16[2,256,2048]{2,1,0:T(8,128)(2,1)}, bf16[3,704,256]{2,1,0:T(8,128)(2,1)}, bf16[3,704,256]{2,1,0:T(8,128)(2,1)}, bf16[512,2048]{1,0:T(8,128)(2,1)}) custom-call(bf16[512,2048]{1,0:T(8,128)(2,1)S(1)} %bitcast.22, bf16[704,2048]{1,0:T(8,128)(2,1)S(1)} %bitcast.25, bf16[704,2048]{1,0:T(8,128)(2,1)S(1)} %bitcast.27, ...), custom_call_target="tpu_custom_call" | custom-call | flops 8858370048 | bytes 17301504 | tf_op jit(solution)/shard_map/expert/pallas_call | solution.py:152
  57.5 0.0 copy-start.5
  57.5 1.6 %collective-permute-start.3 = (bf16[2,256,2048]{2,1,0:T(8,128)(2,1)}, bf16[2,256,2048]{2,1,0:T(8,128)(2,1)}, u32[]{:S(2)}, u32[]{:S(2)}) collective-permute-start(bf16[2,256,2048]{2,1,0:T(8,128)(2,1)} %get-tuple-element.30.rows_ref), channel_id=1, source_target_pairs={{0,1},{1,0},{2,3},{3,2},{4,5},{5,4},{6,7},{7,6},{8,9},{9,8},{10,11... | collective-permute-start | bytes 6291464 | tf_op jit(solution)/shard_map/ppermute | solution.py:270
  59.2 4.7 %all-to-all-start.1 = ((bf16[64,8,2048]{2,1,0:T(8,128)(2,1)}), bf16[64,8,2048]{2,1,0:T(8,128)(2,1)S(1)}, u32[]{:S(2)}, u32[]{:S(2)}) async-start(bf16[64,8,2048]{2,1,0:T(8,128)(2,1)} %bitcast.28), calls=%async_computation.1 | async-start | bytes 4194304 | tf_op jit(solution)/shard_map/all_to_all | solution.py:266
  63.9 0.0 copy-done.5
  63.9 0.2 collective-permute-start.4
  64.1 1.3 %select.1 = (bf16[96,512]{1,0:T(8,128)(2,1)S(1)}, s32[512,32]{1,0:T(8,128)S(1)}) custom-call(s32[6,32]{1,0:T(8,128)} %bitcast.32, f32[6,32]{1,0:T(8,128)} %bitcast.34, bf16[512,2048]{1,0:T(8,128)(2,1)} %get-tuple-element.27.after_hbm), custom_call_target="tpu_custom_call" | custom-call | flops 1048576 | bytes 163840 | tf_op jit(solution)/shard_map/select/pallas_call | solution.py:216
  65.4 1.4 %collective-permute-done.4.act2_ref = bf16[3,704,256]{2,1,0:T(8,128)(2,1)} collective-permute-done((bf16[3,704,256]{2,1,0:T(8,128)(2,1)S(1)}, bf16[3,704,256]{2,1,0:T(8,128)(2,1)}, u32[]{:S(2)}, u32[]{:S(2)}) %collective-permute-start.4) | collective-permute-done | bytes 1081376 | tf_op jit(solution)/shard_map/ppermute | solution.py:270
  66.8 0.0 collective-permute-done.3.rows2_ref
  66.8 0.0 copy-start.3
  66.8 1.6 %copy-done.3 = bf16[2,256,2048]{2,1,0:T(8,128)(2,1)S(1)} copy-done((bf16[2,256,2048]{2,1,0:T(8,128)(2,1)S(1)}, bf16[2,256,2048]{2,1,0:T(8,128)(2,1)}, u32[]{:S(2)}) %copy-start.3) | copy-done | bytes 2097176
  68.4 0.0 copy-start.4
  68.4 1.2 %copy-done.4 = bf16[3,704,256]{2,1,0:T(8,128)(2,1)S(1)} copy-done((bf16[3,704,256]{2,1,0:T(8,128)(2,1)S(1)}, bf16[3,704,256]{2,1,0:T(8,128)(2,1)}, u32[]{:S(2)}) %copy-start.4) | copy-done | bytes 1081368
  69.6 0.0 copy-start
  69.6 9.9 %weight_grads.1 = (bf16[704,2048]{1,0:T(8,128)(2,1)}, bf16[704,2048]{1,0:T(8,128)(2,1)}, bf16[704,2048]{1,0:T(8,128)(2,1)}) custom-call(bf16[2,256,2048]{2,1,0:T(8,128)(2,1)S(1)} %copy-done.3, bf16[3,704,256]{2,1,0:T(8,128)(2,1)S(1)} %copy-done.4, bf16[2,256,2048]{2,1,0:T(8,128)(2,1)} %collective-permute-done.3.rows2_ref, ...), custom_call_target="tpu_custom_call" | custom-call | flops 4429185024 | bytes 8650752 | tf_op jit(solution)/shard_map/weight_grads/pallas_call | solution.py:183
  79.5 14.8 %all-to-all-done.1 = bf16[64,8,2048]{2,1,0:T(8,128)(2,1)S(1)} async-done(((bf16[64,8,2048]{2,1,0:T(8,128)(2,1)}), bf16[64,8,2048]{2,1,0:T(8,128)(2,1)S(1)}, u32[]{:S(2)}, u32[]{:S(2)}) %all-to-all-start.1) | async-done | bytes 2097184 | tf_op jit(solution)/shard_map/all_to_all | solution.py:266
  94.2 0.0 copy-done
  94.3 1.7 %combine.1 = (bf16[32,2048]{1,0:T(8,128)(2,1)}, bf16[32,2048]{1,0:T(8,128)(2,1)}, f32[6,32]{1,0:T(8,128)}) custom-call(bf16[96,512]{1,0:T(8,128)(2,1)S(1)} %get-tuple-element.36.pick_ref, s32[512,32]{1,0:T(8,128)S(1)} %get-tuple-element.37.choice_ref, bf16[32,2048]{1,0:T(8,128)(2,1)S(1)} %copy-done, bf16[512,2048]{1,0:T(8,128)(2,1)S(1)} %bitcast.21), custom_call_target="tpu_custom_call" | custom-call | tf_op jit(solution)/shard_map/combine/pallas_call | solution.py:247
Async XLA Ops:
  0.6 45.9 %collective-permute-start = (bf16[704,2048]{1,0:T(8,128)(2,1)}, bf16[704,2048]{1,0:T(8,128)(2,1)S(1)}, u32[]{:S(2)}, u32[]{:S(2)}) collective-permute-start(bf16[704,2048]{1,0:T(8,128)(2,1)} %bitcast.24), channel_id=1, source_target_pairs={{0,1},{1,0},{2,3},{3,2},{4,5},{5,4},{6,7},{7,6},{8,9},{9,8},{10,11... | collective-permute-start | bytes 8650760 | tf_op jit(solution)/shard_map/ppermute | solution.py:270
  2.1 44.4 %collective-permute-start.1 = (bf16[704,2048]{1,0:T(8,128)(2,1)}, bf16[704,2048]{1,0:T(8,128)(2,1)S(1)}, u32[]{:S(2)}, u32[]{:S(2)}) collective-permute-start(bf16[704,2048]{1,0:T(8,128)(2,1)} %bitcast.26), channel_id=1, source_target_pairs={{0,1},{1,0},{2,3},{3,2},{4,5},{5,4},{6,7},{7,6},{8,9},{9,8},{10,11... | collective-permute-start | bytes 8650760 | tf_op jit(solution)/shard_map/ppermute | solution.py:270
  2.2 44.3 %collective-permute-start.2 = (bf16[704,2048]{1,0:T(8,128)(2,1)}, bf16[704,2048]{1,0:T(8,128)(2,1)S(1)}, u32[]{:S(2)}, u32[]{:S(2)}) collective-permute-start(bf16[704,2048]{1,0:T(8,128)(2,1)} %bitcast.29), channel_id=1, source_target_pairs={{0,1},{1,0},{2,3},{3,2},{4,5},{5,4},{6,7},{7,6},{8,9},{9,8},{10,11... | collective-permute-start | bytes 8650760 | tf_op jit(solution)/shard_map/ppermute | solution.py:270
  2.6 43.9 %copy-start.2 = (bf16[1,2048,704]{1,2,0:T(8,128)(2,1)S(1)}, bf16[1,2048,704]{1,2,0:T(8,128)(2,1)}, u32[]{:S(2)}) copy-start(bf16[1,2048,704]{1,2,0:T(8,128)(2,1)} %param.12) | copy-start | bytes 8650756
  5.1 41.5 %copy-start.1 = (bf16[1,2048,704]{1,2,0:T(8,128)(2,1)S(1)}, bf16[1,2048,704]{1,2,0:T(8,128)(2,1)}, u32[]{:S(2)}) copy-start(bf16[1,2048,704]{1,2,0:T(8,128)(2,1)} %param.11) | copy-start | bytes 8650756
  57.5 6.4 %copy-start.5 = (bf16[3,704,256]{2,1,0:T(8,128)(2,1)S(1)}, bf16[3,704,256]{2,1,0:T(8,128)(2,1)}, u32[]{:S(2)}) copy-start(bf16[3,704,256]{2,1,0:T(8,128)(2,1)} %get-tuple-element.32) | copy-start | bytes 3244036
  57.5 9.3 %collective-permute-start.3 = (bf16[2,256,2048]{2,1,0:T(8,128)(2,1)}, bf16[2,256,2048]{2,1,0:T(8,128)(2,1)}, u32[]{:S(2)}, u32[]{:S(2)}) collective-permute-start(bf16[2,256,2048]{2,1,0:T(8,128)(2,1)} %get-tuple-element.30.rows_ref), channel_id=1, source_target_pairs={{0,1},{1,0},{2,3},{3,2},{4,5},{5,4},{6,7},{7,6},{8,9},{9,8},{10,11... | collective-permute-start | bytes 6291464 | tf_op jit(solution)/shard_map/ppermute | solution.py:270
  59.2 35.1 %all-to-all-start.1 = ((bf16[64,8,2048]{2,1,0:T(8,128)(2,1)}), bf16[64,8,2048]{2,1,0:T(8,128)(2,1)S(1)}, u32[]{:S(2)}, u32[]{:S(2)}) async-start(bf16[64,8,2048]{2,1,0:T(8,128)(2,1)} %bitcast.28), calls=%async_computation.1 | async-start | bytes 4194304 | tf_op jit(solution)/shard_map/all_to_all | solution.py:266
  63.9 2.9 %collective-permute-start.4 = (bf16[3,704,256]{2,1,0:T(8,128)(2,1)S(1)}, bf16[3,704,256]{2,1,0:T(8,128)(2,1)}, u32[]{:S(2)}, u32[]{:S(2)}) collective-permute-start(bf16[3,704,256]{2,1,0:T(8,128)(2,1)S(1)} %copy-done.5), channel_id=1, source_target_pairs={{0,1},{1,0},{2,3},{3,2},{4,5},{5,4},{6,7},{7,6},{8,9},{9,8},{10,11... | collective-permute-start | bytes 3244040 | tf_op jit(solution)/shard_map/ppermute | solution.py:270
  66.8 1.6 %copy-start.3 = (bf16[2,256,2048]{2,1,0:T(8,128)(2,1)S(1)}, bf16[2,256,2048]{2,1,0:T(8,128)(2,1)}, u32[]{:S(2)}) copy-start(bf16[2,256,2048]{2,1,0:T(8,128)(2,1)} %get-tuple-element.30.rows_ref) | copy-start | bytes 6291460
  68.4 1.2 %copy-start.4 = (bf16[3,704,256]{2,1,0:T(8,128)(2,1)S(1)}, bf16[3,704,256]{2,1,0:T(8,128)(2,1)}, u32[]{:S(2)}) copy-start(bf16[3,704,256]{2,1,0:T(8,128)(2,1)} %get-tuple-element.31.act_ref) | copy-start | bytes 3244036
  69.6 24.6 %copy-start = (bf16[32,2048]{1,0:T(8,128)(2,1)S(1)}, bf16[32,2048]{1,0:T(8,128)(2,1)}, u32[]{:S(2)}) copy-start(bf16[32,2048]{1,0:T(8,128)(2,1)} %cot_ref.1) | copy-start | bytes 393220
